TPU v7x, 32 devices: a whole 2x2x4 slice. The times are simulated.
32 devices in a mesh: dp: 16 (over z, y, x), tensor: 2 (over core).
Axes of the slice: x: 2, y: 2, z: 4, core: 2. Of those that a mesh axis runs over, the one named last changes fastest.
Arguments:
- inputs: bfloat16 [64, 1024, 512], P('dp', 'tensor'), may hold values from -6 to 6
- initial_state: float32 [64, 1024], P('dp', 'tensor'), may hold values from -6 to 6
- first_gain: float32 [512], replicated, may hold values from 0.1 to 1.9
- causal_filter: float32 [4, 512], replicated, may hold values from -3 to 3
- mixer_weight: bfloat16 [512, 2, 1024], P(None, None, 'tensor'), may hold values from -0.25 to 0.25
- gate_bias: float32 [1024], P('tensor'), may hold values from -6 to 2
- readout_weight: bfloat16 [1024, 512], P('tensor'), may hold values from -0.1875 to 0.1875
- second_gain: float32 [512], replicated, may hold values from 0.1 to 1.9
- up_weight: bfloat16 [512, 2048], P(None, 'tensor'), may hold values from -0.25 to 0.25
- up_bias: float32 [2048], P('tensor'), may hold values from -3 to 3
- down_weight: bfloat16 [2048, 512], P('tensor'), may hold values from -0.1875 to 0.1875
- cotangent: bfloat16 [64, 1024, 512], P('dp', 'tensor'), may hold values from -6 to 6
Outputs:
- block_output: bfloat16 [64, 1024, 512], P('dp', 'tensor')
- input_gradient: bfloat16 [64, 1024, 512], P('dp', 'tensor')
- state_gradient: float32 [64, 1024], P('dp', 'tensor')
- first_gain_gradient: float32 [512], replicated
- filter_gradient: float32 [4, 512], replicated
- mixer_gradient: float32 [512, 2, 1024], P(None, None, 'tensor')
- gate_bias_gradient: float32 [1024], P('tensor')
- readout_gradient: float32 [1024, 512], P('tensor')
- second_gain_gradient: float32 [512], replicated
- up_weight_gradient: float32 [512, 2048], P(None, 'tensor')
- up_bias_gradient: float32 [2048], P('tensor')
- down_weight_gradient: float32 [2048, 512], P('tensor')
All inputs are finite; a program needn't handle non-finite values.
Results may differ from a plain program's by a relative error of at most 0.0075.
Values may be sent and summed in bfloat16 or wider, within the bound.
No kernel may reach another device: no remote copies, remote signals or barrier semaphores. Data moves between devices by JAX's collectives and lax.ppermute only.
A program may use at most 256 MiB of HBM per device.

v0:
```python
import math

import jax
import jax.numpy as jnp
from jax import lax
from jax.sharding import PartitionSpec as P

epsilon = 1e-06


def shifted(block, axis, distance):
    devices = range(lax.axis_size(axis))
    route = [(i - distance, i) for i in devices if i - distance in devices]
    return lax.ppermute(block, axis, route)


def normalize(values, gain):
    return values * lax.rsqrt(jnp.mean(values * values, axis=-1, keepdims=True) + epsilon) * gain


def gating(gate_input, candidate_input):
    return (
        jax.nn.sigmoid(-gate_input),
        jax.nn.sigmoid(gate_input) * jax.nn.softplus(candidate_input),
    )


def combine(earlier, later):
    return (earlier[0] * later[0], later[0] * earlier[1] + later[1])


def contract(left, right, left_dim, right_dim):
    return lax.dot_general(
        left, right, (((left_dim,), (right_dim,)), ((), ())), preferred_element_type=jnp.float32
    )


def contract_rows(left, right):
    return lax.dot_general(
        left, right, (((0, 1), (0, 1)), ((), ())), preferred_element_type=jnp.float32
    )


def chain_scan(factor_in, offset_in, reverse):
    row_total = factor_in.shape[0]
    block_len = math.gcd(row_total, 8)
    block_count = row_total // block_len
    rest = factor_in.shape[1:]
    factor_blocks = factor_in.reshape((block_count, block_len) + rest)
    offset_blocks = offset_in.reshape((block_count, block_len) + rest)
    order = range(block_len - 1, -1, -1) if reverse else range(block_len)
    running_factor = jnp.ones((block_count,) + rest, jnp.float32)
    running_offset = jnp.zeros((block_count,) + rest, jnp.float32)
    factor_list = [None] * block_len
    offset_list = [None] * block_len
    for position in order:
        running_factor = factor_blocks[:, position] * running_factor
        running_offset = factor_blocks[:, position] * running_offset + offset_blocks[:, position]
        factor_list[position] = running_factor
        offset_list[position] = running_offset
    inner_factor = jnp.stack(factor_list, axis=1)
    inner_offset = jnp.stack(offset_list, axis=1)
    whole_factor, whole_offset = lax.associative_scan(
        combine, (running_factor, running_offset), reverse=reverse, axis=0
    )
    ones_row = jnp.ones((1,) + rest, jnp.float32)
    zeros_row = jnp.zeros((1,) + rest, jnp.float32)
    if reverse:
        enter_factor = jnp.concatenate([whole_factor[1:], ones_row], axis=0)
        enter_offset = jnp.concatenate([whole_offset[1:], zeros_row], axis=0)
    else:
        enter_factor = jnp.concatenate([ones_row, whole_factor[:-1]], axis=0)
        enter_offset = jnp.concatenate([zeros_row, whole_offset[:-1]], axis=0)
    factors = inner_factor * enter_factor[:, None]
    offsets = inner_factor * enter_offset[:, None] + inner_offset
    return (factors.reshape(factor_in.shape), offsets.reshape(factor_in.shape))


def local(
    inputs,
    initial_state,
    first_gain,
    causal_filter,
    mixer_weight,
    gate_bias,
    readout_weight,
    second_gain,
    up_weight,
    up_bias,
    down_weight,
    cotangent,
):
    windows = inputs.shape[0]
    row_count = inputs.shape[1]
    features = inputs.shape[2]
    tap_count = causal_filter.shape[0]
    local_rows = jnp.swapaxes(inputs, 0, 1).astype(jnp.float32)
    tangent_rows = jnp.swapaxes(cotangent, 0, 1)
    normed, first_pull = jax.vjp(normalize, local_rows, first_gain)
    rim_rows = shifted(normed[row_count - tap_count + 1 :], "tensor", 1)
    padded = jnp.concatenate([rim_rows, normed], axis=0)
    filtered = sum(
        (
            causal_filter[tap_index] * padded[tap_index : tap_index + row_count]
            for tap_index in range(tap_count)
        )
    ).astype(jnp.bfloat16)
    filtered_all = lax.all_gather(filtered, "tensor", axis=0, tiled=True)
    mixer_full, readout_full, up_full, down_full = (
        mixer_weight,
        readout_weight,
        up_weight,
        down_weight,
    )
    gate_bias_full, up_bias_full, state_start = (gate_bias, up_bias, initial_state)
    channels = mixer_full.shape[2]
    flat_mixer = mixer_full.reshape(features, 2 * channels)
    projected = jnp.dot(filtered_all, flat_mixer, preferred_element_type=jnp.float32).reshape(
        filtered_all.shape[0], windows, 2, channels
    )
    gate_input = projected[:, :, 0] + gate_bias_full
    candidate_input = projected[:, :, 1]
    (decays, inject), gate_pull = jax.vjp(gating, gate_input, candidate_input)
    factors, offsets = chain_scan(decays, inject, False)
    states = factors * state_start + offsets
    previous = jnp.concatenate([state_start[None], states[:-1]], axis=0)
    states_low = states.astype(jnp.bfloat16)
    mixed_out = lax.psum_scatter(
        jnp.dot(states_low, readout_full, preferred_element_type=jnp.float32),
        "tensor",
        scatter_dimension=0,
        tiled=True,
    )
    middle = local_rows + mixed_out
    normed_two, second_pull = jax.vjp(normalize, middle, second_gain)
    normed_low = normed_two.astype(jnp.bfloat16)
    second_rows = lax.all_gather(normed_low, "tensor", axis=0, tiled=True)
    hidden = jnp.dot(second_rows, up_full, preferred_element_type=jnp.float32) + up_bias_full
    activation, gelu_pull = jax.vjp(jax.nn.gelu, hidden)
    activation_low = activation.astype(jnp.bfloat16)
    down_out = lax.psum_scatter(
        jnp.dot(activation_low, down_full, preferred_element_type=jnp.float32),
        "tensor",
        scatter_dimension=0,
        tiled=True,
    )
    tangent_all = lax.all_gather(tangent_rows, "tensor", axis=0, tiled=True)
    block_output = jnp.swapaxes((middle + down_out).astype(jnp.bfloat16), 0, 1)
    back_activation = contract(tangent_all, down_full, 2, 1)
    down_gradient = contract_rows(activation_low, tangent_all)
    back_hidden = gelu_pull(back_activation)[0].astype(jnp.bfloat16)
    up_bias_gradient = jnp.sum(back_hidden, axis=(0, 1), dtype=jnp.float32)
    up_gradient = contract_rows(second_rows, back_hidden)
    back_normed_two = lax.psum_scatter(
        contract(back_hidden, up_full, 2, 1), "tensor", scatter_dimension=0, tiled=True
    )
    back_middle_norm, second_gain_part = second_pull(back_normed_two)
    back_middle = tangent_rows.astype(jnp.float32) + back_middle_norm
    back_low_rows = back_middle.astype(jnp.bfloat16)
    back_mixed = lax.all_gather(back_low_rows, "tensor", axis=0, tiled=True)
    back_states = contract(back_mixed, readout_full, 2, 1)
    readout_gradient = contract_rows(states_low, back_mixed)
    following = jnp.concatenate([decays[1:], jnp.ones_like(decays[:1])], axis=0)
    multiplier, carried_local = chain_scan(following, back_states, True)
    state_gradient = decays[0] * carried_local[0]
    back_gate, back_candidate = gate_pull((carried_local * previous, carried_local))
    back_project = (
        jnp.stack([back_gate, back_candidate], axis=2)
        .astype(jnp.bfloat16)
        .reshape(back_gate.shape[0], windows, 2 * channels)
    )
    gate_bias_gradient = jnp.sum(back_project[:, :, :channels], axis=(0, 1), dtype=jnp.float32)
    mixer_gradient = contract_rows(filtered_all, back_project).reshape(features, 2, channels)
    back_filtered = lax.psum_scatter(
        contract(back_project, flat_mixer, 2, 1), "tensor", scatter_dimension=0, tiled=True
    )
    ahead_rows = shifted(back_filtered[: tap_count - 1], "tensor", -1)
    extended = jnp.concatenate([back_filtered, ahead_rows], axis=0)
    back_normed = sum(
        (
            causal_filter[tap_index]
            * extended[tap_count - 1 - tap_index : tap_count - 1 - tap_index + row_count]
            for tap_index in range(tap_count)
        )
    )
    filter_part = jnp.stack(
        [
            jnp.sum(back_filtered * padded[tap_index : tap_index + row_count], axis=(0, 1))
            for tap_index in range(tap_count)
        ]
    )
    back_inputs, first_gain_part = first_pull(back_normed)
    input_gradient = jnp.swapaxes((back_middle + back_inputs).astype(jnp.bfloat16), 0, 1)
    small_sums = lax.psum((first_gain_part, filter_part, second_gain_part), ("dp", "tensor"))
    joint_sums = lax.psum(
        (
            mixer_gradient,
            gate_bias_gradient,
            readout_gradient,
            up_gradient,
            up_bias_gradient,
            down_gradient,
        ),
        "dp",
    )
    mixer_sums = joint_sums[:3]
    feed_sums = joint_sums[3:]
    return (
        block_output,
        input_gradient,
        state_gradient,
        small_sums[0],
        small_sums[1],
        mixer_sums[0],
        mixer_sums[1],
        mixer_sums[2],
        small_sums[2],
        feed_sums[0],
        feed_sums[1],
        feed_sums[2],
    )


def solution(mesh):
    return jax.shard_map(
        local,
        mesh=mesh,
        in_specs=(
            P("dp", "tensor", None),
            P("dp", "tensor"),
            P(),
            P(),
            P(None, None, "tensor"),
            P("tensor"),
            P("tensor", None),
            P(),
            P(None, "tensor"),
            P("tensor"),
            P("tensor", None),
            P("dp", "tensor", None),
        ),
        out_specs=(
            P("dp", "tensor", None),
            P("dp", "tensor", None),
            P("dp", "tensor"),
            P(),
            P(),
            P(None, None, "tensor"),
            P("tensor"),
            P("tensor", None),
            P(),
            P(None, "tensor"),
            P("tensor"),
            P("tensor", None),
        ),
        check_vma=False,
    )
```

profile of v0, /device:TPU:0, one launch (start us, length us, event | category | flops | bytes accessed | tf_op | source)
XLA Modules:
  0.0 890.5 jit_solution(10419439540146464429)
XLA Ops:
  20.0 14.9 %all-gather.5.cloned.1.call-done = bf16[1024,4,512]{2,0,1:T(8,128)(2,1)} async-done(((bf16[512,4,512]{2,0,1:T(8,128)(2,1)}), bf16[1024,4,512]{2,0,1:T(8,128)(2,1)}) %all-gather.5.cloned.1.call-update) | async-done | bytes 4194320 | tf_op jit(solution)/shard_map/all_gather | solution.py:108
  34.9 6.6 fusion.29
  41.5 7.3 slice_bitcast_fusion.2
  48.8 3.5 copy-done.4
  52.3 14.1 %add_divide_fusion.1 = (f32[128,8,4,512]{3,0,2,1:T(8,128)S(1)}, f32[128,8,4,512]{3,0,2,1:T(8,128)S(1)}) fusion(f32[128,8,4,512]{3,1,0,2:T(8,128)} %get-tuple-element.101, f32[512]{0:T(512)S(1)} %copy-done.53, f32[128,8,4,512]{3,1,0,2:T(8,128)} %get-tuple-element.102), kind=kLoop, calls=%fused_computation.44 | loop fusion | flops 27262976 | bytes 33556480 | tf_op jit(solution)/shard_map/jvp()/div | solution.py:23
  74.7 4.4 fusion.83
  100.6 4.3 pad.349
  110.1 3.4 fusion.92
  113.5 3.8 constant_dynamic-update-slice_fusion.1
  130.1 7.6 broadcast_multiply_fusion
  137.6 9.3 %bitcast_add_fusion.1 = f32[1024,4,512]{2,0,1:T(8,128)S(1)} fusion(f32[128,8,4,512]{3,0,2,1:T(8,128)S(1)} %get-tuple-element.128, f32[128,8,4,512]{3,0,2,1:T(8,128)S(1)} %get-tuple-element.127, f32[4,512]{1,0:T(4,128)S(1)} %copy-done.46), kind=kLoop, calls=%fused_computation.36 | loop fusion | flops 4194304 | bytes 25174016 | tf_op jit(solution)/shard_map/add | solution.py:125
  146.9 3.3 copy-done.3
  150.2 5.7 fusion.40
  156.4 17.6 %reduce-scatter.5.cloned.1.call-done = f32[512,4,512]{2,0,1:T(8,128)} async-done(((f32[1024,4,512]{2,0,1:T(8,128)}), f32[512,4,512]{2,0,1:T(8,128)}) %reduce-scatter.5.cloned.1.call-update) | async-done | bytes 4194320 | tf_op jit(solution)/shard_map/reduce_scatter | solution.py:128
  181.3 14.4 %all-gather.7.cloned.1.call-done = bf16[1024,4,512]{2,0,1:T(8,128)(2,1)} async-done(((bf16[512,4,512]{2,0,1:T(8,128)(2,1)}), bf16[1024,4,512]{2,0,1:T(8,128)(2,1)}) %all-gather.7.cloned.1.call-update) | async-done | bytes 4194320 | tf_op jit(solution)/shard_map/all_gather | solution.py:137
  195.7 16.4 %multiply_convert_fusion = (bf16[1024,4,1024]{2,0,1:T(8,128)(2,1)}, f32[1024,4,1024]{2,0,1:T(8,128)}) fusion(f32[1024]{0:T(1024)S(1)} %copy-done.71, bf16[1024,4,512]{2,0,1:T(8,128)(2,1)} %all-gather.7.cloned.1.call-done, bf16[512,1024]{1,0:T(8,128)(2,1)S(1)} %copy-done), kind=kOutput, calls=%fused_computation.15 | convolution fusion | flops 4336910336 | bytes 30412800 | tf_op jit(solution)/shard_map/dot_general | solution.py:138
  212.1 17.8 %convert_reduce_fusion = (f32[1024]{0:T(1024)}, bf16[1024,4,1024]{2,0,1:T(8,128)(2,1)S(1)}) fusion(f32[1024,4,1024]{2,0,1:T(8,128)} %get-tuple-element.190, f32[1024]{0:T(1024)S(1)} %copy-done.71, bf16[1024,4,512]{2,0,1:T(8,128)(2,1)} %all-gather.9.cloned.1.call-done, bf16[1024,512]{1,0:T(8,128)(2,1)S(1)} %copy-done.69), kind=kOutput, calls=%fused_computation.14 | convolution fusion | flops 4391435264 | bytes 30416896 | tf_op jit(solution)/shard_map/dot_general | solution.py:33
  230.0 3.3 copy-done.72
  233.2 6.9 fusion.67
  241.0 4.6 fusion.19
  245.6 3.6 copy-done.13
  250.6 5.8 pad_bitcast_fusion
  257.6 4.2 slice_bitcast_fusion
  261.8 4.8 multiply_reduce_fusion
  270.0 27.5 %fusion.116 = (f32[128,1,4,512]{3,1,0,2:T(1,128)S(1)}, f32[128,1,4,512]{3,1,0,2:T(1,128)S(1)}, f32[128,1,4,512]{3,1,0,2:T(1,128)}, f32[128,1,4,512]{3,1,0,2:T(1,...) fusion(f32[128,8,4,512]{3,1,0,2:T(8,128)} %pad_bitcast_fusion), kind=kLoop, calls=%fused_computation.304 | loop fusion | bytes 16777216 | tf_op jit(solution)/shard_map/slice | solution.py:57
  297.5 10.6 %convolution_bitcast_fusion.3 = f32[512,1024]{1,0:T(8,128)} fusion(bf16[1024,4,512]{2,0,1:T(8,128)(2,1)} %all-gather.7.cloned.1.call-done, bf16[1024,4,1024]{2,0,1:T(8,128)(2,1)} %copy-done.72), kind=kOutput, calls=%fused_computation.98 | convolution fusion | flops 4294967296 | bytes 14680064 | tf_op jit(solution)/shard_map/dot_general | solution.py:39
  308.1 8.3 convolution_bitcast_fusion.2
  316.4 8.0 convolution_bitcast_fusion.1
  324.4 27.5 %fusion.117 = (f32[128,1,4,512]{3,1,0,2:T(1,128)}, f32[128,1,4,512]{3,1,0,2:T(1,128)}, f32[128,1,4,512]{3,1,0,2:T(1,128)}, f32[128,1,4,512]{3,1,0,2:T(1,128)}, f...) fusion(f32[128,8,4,512]{3,1,0,2:T(8,128)} %convolution_bitcast_, ...), kind=kLoop, calls=%fused_computation.305 | loop fusion | bytes 16777216 | tf_op jit(solution)/shard_map/slice | solution.py:58
  351.9 8.4 fusion.63
  360.3 3.3 slice.685
  363.5 3.3 slice.678
  366.8 3.2 slice.676
  371.5 3.3 slice.730
  374.8 3.3 slice.682
  378.0 3.3 slice.680
  381.3 3.2 slice.686
  384.5 3.2 slice.679
  390.9 3.2 slice.683
  426.8 8.7 multiply_dynamic-update-slice_fusion
  435.5 3.2 slice.677
  438.7 3.2 slice.731
  451.5 3.5 pad.170
  460.9 3.8 pad.172
  469.4 4.3 pad.230
  473.6 4.3 pad.350
  480.6 9.1 %slice.733 = f32[127,4,512]{2,0,1:T(8,128)} reverse(f32[127,4,512]{2,0,1:T(8,128)} %slice_add_fusion.4), dimensions={0} | reverse | bytes 2080768 | tf_op jit(solution)/shard_map/slice | solution.py:70
  492.2 4.1 fusion.89
  508.2 12.0 %multiply_add_fusion = f32[128,8,4,512]{3,0,2,1:T(8,128)} fusion(f32[128,8,4,512]{3,0,2,1:T(8,128)} %get-tuple-element.134, f32[128,8,4,512]{3,0,2,1:T(8,128)} %get-tuple-element.133, f32[128,4,512]{2,0,1:T(8,128)S(1)} %copy-done.28), kind=kLoop, calls=%fused_computation.41 | loop fusion | flops 4194304 | bytes 26214400 | tf_op jit(solution)/shard_map/add | solution.py:75
  520.2 20.9 %fusion.8 = (bf16[1024,4,1,512]{3,0,2,1:T(8,128)(2,1)}, bf16[1024,4,1,512]{3,0,2,1:T(8,128)(2,1)}) fusion(f32[1023,4,1,512]{3,0,2,1:T(8,128)} %slice_bitcast_fusion, f32[1,4,1,512]{3,0,2,1:T(1,128)S(1)} %copy-done.47, f32[1024,4,2,512]{3,0,2,1:T(8,128)} %copy-done.4, f32[128,8,4,512]{3,0,2,1:T(8,128)} %multiply_add_fusion, f32[512]{0:T(512)S(1)} %copy-done.54), kind=kLoop, calls=%fused_computation.19 | loop fusion | flops 67108864 | bytes 41945088 | tf_op jit(solution)/shard_map/transpose(jvp())/add_any | solution.py:23
  541.1 7.7 maximum_convert_fusion
  548.8 6.9 fusion.47
  555.9 5.8 fusion.42
  561.8 10.3 %convolution_bitcast_fusion = f32[1024,4,512]{2,0,1:T(8,128)} fusion(bf16[1024,4,2,512]{3,0,2,1:T(8,128)(2,1)} %maximum_convert_fusion, bf16[512,2,512]{2,1,0:T(2,128)(2,1)S(1)} %copy-done.35), kind=kOutput, calls=%fused_computation.88 | convolution fusion | flops 4294967296 | bytes 17825792 | tf_op jit(solution)/shard_map/dot_general | solution.py:33
  573.3 10.5 %fusion.65 = f32[1024,4,512]{2,0,1:T(8,128)} fusion(bf16[1024,4,1024]{2,0,1:T(8,128)(2,1)} %get-tuple-element.189, bf16[1024,512]{1,0:T(8,128)(2,1)S(1)} %copy-done.70), kind=kOutput, calls=%fused_computation.125 | convolution fusion | flops 4294967296 | bytes 17825792 | tf_op jit(solution)/shard_map/dot_general | solution.py:142
  583.9 11.7 %copy.331 = f32[128,8,4,512]{3,1,0,2:T(8,128)} copy(f32[128,8,4,512]{3,0,2,1:T(8,128)} %multiply_add_fusion) | data formatting | bytes 16777216 | tf_op jit(solution)/shard_map/add | solution.py:75
  595.5 11.6 %copy.158 = bf16[1024,4,2,512]{0,3,2,1:T(8,128)(2,1)} copy(bf16[1024,4,2,512]{3,0,2,1:T(8,128)(2,1)} %maximum_convert_fusion) | data formatting | bytes 16777216 | tf_op jit(solution)/shard_map/convert_element_type | solution.py:169
  611.7 44.7 %all-reduce.47 = (f32[512]{0:T(512)}, f32[1024]{0:T(1024)}) all-reduce(f32[512]{0:T(512)S(1)} %convert_reduce_fusion.1, f32[1024]{0:T(1024)S(1)} %copy-done.66), channel_id=1, replica_groups=mesh['dp'=16,'tensor'=2] {'dp'}, use_global_device_ids=true, to_apply=%region_17.18 | all-reduce | flops 1536 | bytes 12288 | tf_op jit(solution)/shard_map/psum | solution.py:195
  656.4 142.2 %all-reduce.51.cloned.1.call-done = (f32[512,2,512]{2,0,1:T(8,128)}, f32[512,512]{1,0:T(8,128)}, f32[512,1024]{1,0:T(8,128)}, f32[1024,512]{1,0:T(8,128)}) async-done(((f32[512,2,512]{2,0,1:T(8,128)}, f32[512,512]{1,0:T(8,128)}, f32[512,1024]{1,0:T(8,128)}, f32[1024,512]{1,0:T(8,128)}), (f32[512,2,512]{2,0,1:T(8,128)}, f32[512,512]{1,0:T(8,128)}, f32[512,1024]{1,0:T(8,128)}, ...) | async-done | bytes 7340048 | tf_op jit(solution)/shard_map/psum | solution.py:195
  798.6 4.5 copy.164
  803.1 13.7 %reduce-scatter.11.cloned.1.call-done = f32[512,4,512]{2,0,1:T(8,128)} async-done(((f32[1024,4,512]{2,0,1:T(8,128)}), f32[512,4,512]{2,0,1:T(8,128)}) %reduce-scatter.11.cloned.1.call-update) | async-done | bytes 4194320 | tf_op jit(solution)/shard_map/reduce_scatter | solution.py:174
  822.3 6.8 multiply_reduce_fusion.4
  829.2 40.7 %all-reduce.46 = (f32[512]{0:T(512)}, f32[4,512]{1,0:T(4,128)}, f32[512]{0:T(512)}) all-reduce(f32[512]{0:T(512)S(1)} %get-tuple-element.69, f32[4,512]{1,0:T(4,128)S(1)} %pad_maximum_fusion.19, f32[512]{0:T(512)S(1)} %copy-done.65), channel_id=1, replica_groups=mesh['dp'=16,'tensor'=2] {'dp','tensor'}, use_global_device_ids=true, to_apply=%region_9.10 | all-reduce | flops 3072 | bytes 24576 | tf_op jit(solution)/shard_map/psum | solution.py:194
  870.0 10.0 %fusion.37 = (bf16[4,512,512]{2,1,0:T(8,128)(2,1)}, bf16[4,512,512]{2,1,0:T(8,128)(2,1)}) fusion(bf16[4,512,512]{2,1,0:T(8,128)(2,1)S(1)} %copy-done.9, f32[512,4,512]{2,0,1:T(8,128)} %get-tuple-element.79, f32[512,4]{0,1:T(4,128)S(1)} %multiply_multiply_fusion.2, f32[512]{0:T(512)S(1)} %copy-done.63, f32[512,4]{0,1:T(4,128)S(1)} %copy-done.42, ...), kind=kLoop, calls=%fused_computation.91 | loop fusion | flops 17825792 | bytes 25202688 | tf_op jit(solution)/shard_map/transpose | solution.py:193
  (407 shorter events, 163.7 us)
Async XLA Ops:
  7.2 188.5 %copy-start = (bf16[512,1024]{1,0:T(8,128)(2,1)S(1)}, bf16[512,1024]{1,0:T(8,128)(2,1)}, u32[]{:S(2)}) copy-start(bf16[512,1024]{1,0:T(8,128)(2,1)} %param.20) | copy-start | bytes 3145732
  7.2 7.4 copy-start.64
  7.2 11.9 %copy-start.34 = (bf16[512,2,512]{2,1,0:T(2,128)(2,1)S(1)}, bf16[512,2,512]{2,1,0:T(2,128)(2,1)}, u32[]{:S(2)}) copy-start(bf16[512,2,512]{2,1,0:T(2,128)(2,1)} %param.16) | copy-start | bytes 3145732
  7.2 27.6 %all-gather.5.cloned.1.call-start = ((), (), s32[]{:S(2)}) async-start(), calls=%async_computation.4 | async-start | bytes 6291456 | tf_op jit(solution)/shard_map/all_gather | solution.py:108
  12.2 3.2 collective-permute-start
  18.9 155.1 %reduce-scatter.5.cloned.1.call-start = ((), (), s32[]{:S(2)}) async-start(), calls=%async_computation.5 | async-start | bytes 12582912 | tf_op jit(solution)/shard_map/reduce_scatter | solution.py:128
  41.5 10.8 %copy-start.4 = (f32[1024,4,2,512]{3,0,2,1:T(8,128)}, f32[1024,4,2,512]{3,0,2,1:T(8,128)S(1)}, u32[]{:S(2)}) copy-start(f32[1024,4,2,512]{3,0,2,1:T(8,128)S(1)} %fusion.29) | copy-start | bytes 50331652
  41.5 10.8 %copy-start.53 = (f32[512]{0:T(512)S(1)}, f32[512]{0:T(512)}, u32[]{:S(2)}) copy-start(f32[512]{0:T(512)} %param.17) | copy-start | bytes 6148
  107.1 10.3 %slice-start = ((s8[8388608]{0:T(1024)(128)(4,1)}), s8[4194304]{0:T(1024)(128)(4,1)S(1)}, s32[]{:S(2)}) async-start(s8[8388608]{0:T(1024)(128)(4,1)} %bitcast.341), calls=%async_computation.13 | async-start | bytes 8388608
  110.1 7.2 slice-start.1
  113.5 7.6 slice-start.4
  130.1 7.6 copy-start.46
  137.6 12.6 %copy-start.31 = (bf16[512,512]{1,0:T(8,128)(2,1)S(1)}, bf16[512,512]{1,0:T(8,128)(2,1)}, u32[]{:S(2)}) copy-start(bf16[512,512]{1,0:T(8,128)(2,1)} %param.18) | copy-start | bytes 1572868
  155.9 18.1 %copy-start.8 = (bf16[4,512,512]{2,1,0:T(8,128)(2,1)S(1)}, bf16[4,512,512]{2,1,0:T(8,128)(2,1)}, u32[]{:S(2)}) copy-start(bf16[4,512,512]{2,1,0:T(8,128)(2,1)} %param.12) | copy-start | bytes 6291460
  155.9 23.0 %copy-start.51 = (f32[512]{0:T(512)S(1)}, f32[512]{0:T(512)}, u32[]{:S(2)}) copy-start(f32[512]{0:T(512)} %param.19) | copy-start | bytes 6148
  155.9 39.8 %copy-start.71 = (f32[1024]{0:T(1024)S(1)}, f32[1024]{0:T(1024)}, u32[]{:S(2)}) copy-start(f32[1024]{0:T(1024)} %param.21) | copy-start | bytes 12292
  155.9 39.8 %all-gather.7.cloned.1.call-start = ((), (), s32[]{:S(2)}) async-start(), calls=%async_computation.6 | async-start | bytes 6291456 | tf_op jit(solution)/shard_map/all_gather | solution.py:137
  180.7 31.5 %all-gather.9.cloned.1.call-start = ((), (), s32[]{:S(2)}) async-start(), calls=%async_computation.8 | async-start | bytes 6291456 | tf_op jit(solution)/shard_map/all_gather | solution.py:147
  181.2 30.9 %copy-start.69 = (bf16[1024,512]{1,0:T(8,128)(2,1)S(1)}, bf16[1024,512]{1,0:T(8,128)(2,1)}, u32[]{:S(2)}) copy-start(bf16[1024,512]{1,0:T(8,128)(2,1)} %param.22) | copy-start | bytes 3145732
  181.2 80.5 %reduce-scatter.9.cloned.1.call-start = ((), (), s32[]{:S(2)}) async-start(), calls=%async_computation.9 | async-start | bytes 12582912 | tf_op jit(solution)/shard_map/reduce_scatter | solution.py:154
  240.1 76.3 %all-gather.11.cloned.1.call-start = ((), (), s32[]{:S(2)}) async-start(), calls=%async_computation.10 | async-start | bytes 6291456 | tf_op jit(solution)/shard_map/all_gather | solution.py:160
  249.2 7.2 slice-start.2
  250.6 7.0 slice-start.3
  257.6 9.0 %copy-start.15 = (bf16[4,512,512]{2,1,0:T(8,128)(2,1)S(1)}, bf16[4,512,512]{2,1,0:T(8,128)(2,1)}, u32[]{:S(2)}) copy-start(bf16[4,512,512]{2,1,0:T(8,128)(2,1)} %param.23) | copy-start | bytes 6291460
  269.9 528.6 %all-reduce.51.cloned.1.call-start = ((), (), s32[]{:S(2)}) async-start(), calls=%async_computation.12 | async-start | bytes 14680064 | tf_op jit(solution)/shard_map/psum | solution.py:195
  297.5 10.6 %copy-start.68 = (bf16[1024,4,512]{2,0,1:T(8,128)(2,1)S(1)}, bf16[1024,4,512]{2,0,1:T(8,128)(2,1)}, u32[]{:S(2)}) copy-start(bf16[1024,4,512]{2,0,1:T(8,128)(2,1)} %all-gather.9.cloned.1.call-done) | copy-start | bytes 12582916
  426.7 15.1 %copy-start.49 = (f32[1,4,512]{2,0,1:T(1,128)S(1)}, f32[1,4,512]{2,0,1:T(1,128)}, u32[]{:S(2)}) copy-start(f32[1,4,512]{2,0,1:T(1,128)} %get-tuple-element.165) | copy-start | bytes 24580
  426.7 15.1 %copy-start.50 = (f32[1,4,512]{2,0,1:T(1,128)S(1)}, f32[1,4,512]{2,0,1:T(1,128)}, u32[]{:S(2)}) copy-start(f32[1,4,512]{2,0,1:T(1,128)} %get-tuple-element.166) | copy-start | bytes 24580
  426.7 17.2 %copy-start.43 = (f32[3,4,512]{2,0,1:T(4,128)S(1)}, f32[3,4,512]{2,0,1:T(4,128)}, u32[]{:S(2)}) copy-start(f32[3,4,512]{2,0,1:T(4,128)} %slice.705) | copy-start | bytes 73732
  426.7 20.1 %copy-start.38 = (f32[7,4,512]{2,0,1:T(8,128)S(1)}, f32[7,4,512]{2,0,1:T(8,128)}, u32[]{:S(2)}) copy-start(f32[7,4,512]{2,0,1:T(8,128)} %slice.699) | copy-start | bytes 172036
  451.5 17.0 %copy-start.48 = (f32[1,4,512]{2,0,1:T(1,128)S(1)}, f32[1,4,512]{2,0,1:T(1,128)}, u32[]{:S(2)}) copy-start(f32[1,4,512]{2,0,1:T(1,128)} %slice.824) | copy-start | bytes 24580
  489.7 6.6 copy-start.27
  489.7 7.6 copy-start.26
  489.7 8.7 copy-start.20
  489.7 8.7 copy-start.21
  489.7 8.7 copy-start.24
  489.7 8.7 copy-start.25
  496.2 6.1 copy-start.17
  496.2 6.1 copy-start.23
  500.2 6.3 copy-start.19
  508.2 12.0 %copy-start.47 = (f32[1,4,1,512]{3,0,2,1:T(1,128)S(1)}, f32[1,4,1,512]{3,0,2,1:T(1,128)}, u32[]{:S(2)}) copy-start(f32[1,4,1,512]{3,0,2,1:T(1,128)} %concatenate.109) | copy-start | bytes 24580
  508.2 12.0 %copy-start.54 = (f32[512]{0:T(512)S(1)}, f32[512]{0:T(512)}, u32[]{:S(2)}) copy-start(f32[512]{0:T(512)} %param.17) | copy-start | bytes 6148
  541.1 7.7 copy-start.18
  548.8 6.9 copy-start.14
  548.8 7.1 copy-start.67
  561.7 255.1 %reduce-scatter.11.cloned.1.call-start = ((), (), s32[]{:S(2)}) async-start(), calls=%async_computation.11 | async-start | bytes 12582912 | tf_op jit(solution)/shard_map/reduce_scatter | solution.py:174
  572.1 297.8 %reduce-scatter.7.cloned.1.call-start = ((), (), s32[]{:S(2)}) async-start(), calls=%async_computation.7 | async-start | bytes 12582912 | tf_op jit(solution)/shard_map/reduce_scatter | solution.py:141
  595.5 16.1 %copy-start.66 = (f32[1024]{0:T(1024)S(1)}, f32[1024]{0:T(1024)}, u32[]{:S(2)}) copy-start(f32[1024]{0:T(1024)} %get-tuple-element.191) | copy-start | bytes 12292
  608.6 213.5 %copy-start.9 = (bf16[4,512,512]{2,1,0:T(8,128)(2,1)S(1)}, bf16[4,512,512]{2,1,0:T(8,128)(2,1)}, u32[]{:S(2)}) copy-start(bf16[4,512,512]{2,1,0:T(8,128)(2,1)} %param.12) | copy-start | bytes 6291460
  608.6 213.6 %copy-start.40 = (f32[3,4,512]{2,0,1:T(4,128)S(1)}, f32[3,4,512]{2,0,1:T(4,128)}, u32[]{:S(2)}) copy-start(f32[3,4,512]{2,0,1:T(4,128)} %copy-done.39) | copy-start | bytes 73732
  608.6 213.6 %copy-start.42 = (f32[512,4]{0,1:T(4,128)S(1)}, f32[512,4]{0,1:T(4,128)}, u32[]{:S(2)}) copy-start(f32[512,4]{0,1:T(4,128)} %copy-done.41) | copy-start | bytes 24580
  608.7 213.6 %copy-start.56 = (f32[1,512]{1,0:T(1,128)S(1)}, f32[1,512]{1,0:T(1,128)}, u32[]{:S(2)}) copy-start(f32[1,512]{1,0:T(1,128)} %copy-done.55) | copy-start | bytes 6148
  608.7 213.6 %copy-start.58 = (f32[1,512]{1,0:T(1,128)S(1)}, f32[1,512]{1,0:T(1,128)}, u32[]{:S(2)}) copy-start(f32[1,512]{1,0:T(1,128)} %copy-done.57) | copy-start | bytes 6148
  608.7 213.6 %copy-start.60 = (f32[1,512]{1,0:T(1,128)S(1)}, f32[1,512]{1,0:T(1,128)}, u32[]{:S(2)}) copy-start(f32[1,512]{1,0:T(1,128)} %copy-done.59) | copy-start | bytes 6148
  608.7 213.6 %copy-start.62 = (f32[1,512]{1,0:T(1,128)S(1)}, f32[1,512]{1,0:T(1,128)}, u32[]{:S(2)}) copy-start(f32[1,512]{1,0:T(1,128)} %copy-done.61) | copy-start | bytes 6148
  608.7 213.6 %copy-start.63 = (f32[512]{0:T(512)S(1)}, f32[512]{0:T(512)}, u32[]{:S(2)}) copy-start(f32[512]{0:T(512)} %param.14) | copy-start | bytes 6148
  817.8 4.4 collective-permute-start.1
  822.3 6.9 copy-start.65
  822.3 47.6 %copy-start.45 = (f32[512,4]{0,1:T(4,128)S(1)}, f32[512,4]{0,1:T(4,128)}, u32[]{:S(2)}) copy-start(f32[512,4]{0,1:T(4,128)} %copy-done.44) | copy-start | bytes 24580
  822.3 47.6 %copy-start.52 = (f32[512]{0:T(512)S(1)}, f32[512]{0:T(512)}, u32[]{:S(2)}) copy-start(f32[512]{0:T(512)} %param.19) | copy-start | bytes 6148
  870.0 10.1 %copy-start.36 = (f32[512,512]{1,0:T(8,128)S(1)}, f32[512,512]{1,0:T(8,128)}, u32[]{:S(2)}) copy-start(f32[512,512]{1,0:T(8,128)} %get-tuple-element.210) | copy-start | bytes 3145732
  870.0 11.0 %copy-start.33 = (f32[512,1024]{1,0:T(8,128)S(1)}, f32[512,1024]{1,0:T(8,128)}, u32[]{:S(2)}) copy-start(f32[512,1024]{1,0:T(8,128)} %get-tuple-element.212) | copy-start | bytes 6291460
  870.0 12.3 %copy-start.32 = (f32[1024,512]{1,0:T(8,128)S(1)}, f32[1024,512]{1,0:T(8,128)}, u32[]{:S(2)}) copy-start(f32[1024,512]{1,0:T(8,128)} %get-tuple-element.214) | copy-start | bytes 6291460
  870.0 13.7 %copy-start.1 = (bf16[512,1024]{1,0:T(8,128)(2,1)S(1)}, bf16[512,1024]{1,0:T(8,128)(2,1)}, u32[]{:S(2)}) copy-start(bf16[512,1024]{1,0:T(8,128)(2,1)} %param.20) | copy-start | bytes 3145732
  (26 other events, 83.6 us)
Sparse Core Ops, SparseCore 0:
  19.0 15.7 all-gather.4
  156.0 17.9 reduce-scatter.4
  180.8 14.8 all-gather.6
  197.2 14.8 all-gather.8
  240.2 17.9 reduce-scatter.8
  270.1 14.7 all-gather.10
  561.8 236.7 all-reduce.50
  801.0 15.7 reduce-scatter.10
  819.1 18.0 reduce-scatter.6
where the time goes:
time: 897 us; the launch traced here: 890 us
  local copies, waits for them, and re-layouts  264 us (29%)
  waiting for transfers between devices  204 us (23%)
  other arithmetic  202 us (23%)
  matrix products  114 us (13%)
  blocking collectives  85.4 us (10%)
  between operations  15.8 us (2%)
    psum x1, waiting for transfers between devices, local(): lax.psum((mixer_gradient, gate_bias_gradient, readout_gradient, up_gradie...  142 us
    slice x89, local copies, waits for them, and re-layouts, chain_scan(): lax.associative_scan(combine, (running_factor, running_offset), reverse=r...  73.3 us
    unnamed x174, local copies, waits for them, and re-layouts  56.5 us
    psum x1, blocking collectives, local(): lax.psum((mixer_gradient, gate_bias_gradient, readout_gradient, up_gradie...  44.7 us
    dot_general x4, matrix products, contract(): lax.dot_general(left, right, (((left_dim,), (right_dim,)), ((), ())), pre...  43 us
    psum x1, blocking collectives, local(): lax.psum((first_gain_part, filter_part, second_gain_part), ('dp', 'tensor'))  40.7 us
    unnamed x20, other arithmetic  34.6 us
    dot_general x4, matrix products, contract_rows(): lax.dot_general(left, right, (((0, 1), (0, 1)), ((), ())), preferred_elem...  31.6 us
  transfers between devices with their start and end apart: 11, of which 6 were waited for; matrix products, arithmetic and copies ran while one was open for 16% of the time, Pallas kernels for 0%

commit v1 on v0

v1 whole, which is shorter than its diff:
```python
import functools
import math

import jax
import jax.numpy as jnp
from jax import lax
from jax.experimental import pallas as pl
from jax.experimental.pallas import tpu as pltpu
from jax.sharding import PartitionSpec as P

epsilon = 1e-06
low = jnp.bfloat16
wide = jnp.float32
root = math.sqrt(2.0 / math.pi)
cubic = 0.044715
MIB = 1 << 20


def mm(left, right):
    return lax.dot_general(left, right, (((1,), (0,)), ((), ())), preferred_element_type=wide)


def mm_nt(left, right):
    return lax.dot_general(left, right, (((1,), (1,)), ((), ())), preferred_element_type=wide)


def mm_tn(left, right):
    return lax.dot_general(left, right, (((0,), (0,)), ((), ())), preferred_element_type=wide)


def params(mib, grid):
    return pltpu.CompilerParams(
        vmem_limit_bytes=mib * MIB, dimension_semantics=("arbitrary",) * grid
    )


def cost(macs, moved, curves=0):
    return pl.CostEstimate(flops=2 * macs, bytes_accessed=moved, transcendentals=curves)


def whole(array):
    rank = array.ndim
    return pl.BlockSpec(array.shape, lambda *_: (0,) * rank)


def rows_of(tile, width, lanes=8):
    return lax.broadcasted_iota(jnp.int32, (lanes, width), 0)


def forward_kernel(
    core, own, got, gain, taps, mixer_own, mixer_other, bias, start, read_own, read_other,
    gain_two, filtered_out, decay_out, gate_out, cand_out, state_out, middle_out, normed_out,
    rim, gates, cands, carry,
):
    half_chunks = pl.num_programs(1) // 2
    step = pl.program_id(1)
    rows = own.shape[1]
    width = own.shape[2]
    tap_count = taps.shape[0]
    mine = step // half_chunks == core[0]
    x = jnp.where(mine, own[0], got[0]).astype(wide)
    scale = lax.rsqrt(jnp.mean(x * x, axis=-1, keepdims=True) + epsilon)
    normed = x * scale * gain[...]

    @pl.when(step == 0)
    def _():
        rim[0:8, :] = jnp.zeros((8, width), wide)
        carry[...] = jnp.broadcast_to(start[0], carry.shape)

    rim[8 : 8 + rows, :] = normed
    total = taps[0:1, :] * rim[9 - tap_count : 9 - tap_count + rows, :]
    for tap in range(1, tap_count):
        begin = 9 - tap_count + tap
        total = total + taps[tap : tap + 1, :] * rim[begin : begin + rows, :]
    rim[0:8, :] = normed[rows - 8 :, :]
    filtered = total.astype(low)
    filtered_out[...] = filtered
    channels = read_own.shape[0]
    for at, weight in ((0, mixer_own), (1, mixer_other)):
        lanes = slice(at * channels, (at + 1) * channels)
        gates[:, lanes] = mm(filtered, weight[:, :channels]) + bias[:, lanes]
        cands[:, lanes] = mm(filtered, weight[:, channels:])

    group = min(channels, 256)
    place = rows_of(8, group)

    def sweep(index, _):
        base = pl.multiple_of(index * 16, 16)
        for lane in range(0, 2 * channels, group):
            lanes = slice(lane, lane + group)
            state = carry[:, lanes]
            kept = []
            for sub in (0, 8):
                g = gates[pl.ds(base + sub, 8), lanes]
                c = cands[pl.ds(base + sub, 8), lanes]
                t = 0.5 * jnp.tanh(0.5 * g)
                decay = 0.5 - t
                opened = 0.5 + t
                soft = jnp.maximum(c, 0.0) + jnp.log1p(jnp.exp(-jnp.abs(c)))
                a = decay
                b = opened * soft
                for hop in (1, 2, 4):
                    inside = place >= hop
                    a_back = jnp.where(inside, pltpu.roll(a, hop, 0), 1.0)
                    b_back = jnp.where(inside, pltpu.roll(b, hop, 0), 0.0)
                    b = a * b_back + b
                    a = a * a_back
                h = a * state + b
                before = jnp.where(place >= 1, pltpu.roll(h, 1, 0), state)
                state = jnp.broadcast_to(h[7:8, :], h.shape)
                decay_out[pl.ds(base + sub, 8), lanes] = decay
                kept.append(
                    (
                        decay * opened * (soft - before),
                        opened * (0.5 + 0.5 * jnp.tanh(0.5 * c)),
                        h,
                    )
                )
            carry[:, lanes] = state
            for ref, parts in zip((gate_out, cand_out, state_out), zip(*kept)):
                ref[pl.ds(base, 16), lanes] = jnp.concatenate(parts, axis=0).astype(low)
        return 0

    lax.fori_loop(0, rows // 16, sweep, 0)
    mixed = mm(state_out[:, :channels], read_own[...]) + mm(
        state_out[:, channels:], read_other[...]
    )
    middle = x + mixed
    middle_out[...] = middle
    scale_two = lax.rsqrt(jnp.mean(middle * middle, axis=-1, keepdims=True) + epsilon)
    normed_out[...] = (middle * scale_two * gain_two[...]).astype(low)


def halves_specs(chunk, width, windows, halves):
    return (
        pl.BlockSpec(
            (1, chunk, width), lambda w, t, core: (windows * core[0] + w, t % halves, 0)
        ),
        pl.BlockSpec((1, chunk, width), lambda w, t, core: (w, t % halves, 0)),
    )


def fixed(array):
    rank = array.ndim
    return pl.BlockSpec(array.shape, lambda w, t, core: (0,) * rank)


def forward(core, inputs, got, gain, taps, mixers, bias, start, reads, gain_two):
    windows, half, width = got.shape
    channels = reads[0].shape[0]
    chunk = math.gcd(half, 256)
    halves = half // chunk
    steps = 2 * halves
    rows = 2 * half * windows
    row = lambda lanes: pl.BlockSpec((chunk, lanes), lambda w, t, core: (w * steps + t, 0))
    out = lambda lanes, dtype: jax.ShapeDtypeStruct((rows, lanes), dtype)
    return pl.pallas_call(
        forward_kernel,
        grid_spec=pltpu.PrefetchScalarGridSpec(
            num_scalar_prefetch=1,
            grid=(windows, steps),
            in_specs=[
                *halves_specs(chunk, width, windows, halves),
                fixed(gain),
                fixed(taps),
                fixed(mixers[0]),
                fixed(mixers[1]),
                fixed(bias),
                pl.BlockSpec((1, 1, 2 * channels), lambda w, t, core: (w, 0, 0)),
                fixed(reads[0]),
                fixed(reads[1]),
                fixed(gain_two),
            ],
            out_specs=[
                row(width),
                row(2 * channels),
                row(2 * channels),
                row(2 * channels),
                row(2 * channels),
                row(width),
                row(width),
            ],
            scratch_shapes=[
                pltpu.VMEM((chunk + 8, width), wide),
                pltpu.VMEM((chunk, 2 * channels), wide),
                pltpu.VMEM((chunk, 2 * channels), wide),
                pltpu.VMEM((8, 2 * channels), wide),
            ],
        ),
        out_shape=[
            out(width, low),
            out(2 * channels, wide),
            out(2 * channels, low),
            out(2 * channels, low),
            out(2 * channels, low),
            out(width, wide),
            out(width, low),
        ],
        compiler_params=params(48, 2),
        cost_estimate=cost(rows * width * channels * 6, rows * channels * 24, rows * channels * 8),
        name="forward_mixer",
    )(core, inputs, got, gain, taps, *mixers, bias, start, *reads, gain_two)


def feed_kernel(
    core, own, got, normed, up_own, up_other, bias, down_own, down_other,
    tangent_out, active_out, back_out, bias_out,
):
    half_chunks = pl.num_programs(1) // 2
    step = pl.program_id(1)
    tangent = jnp.where(step // half_chunks == core[0], own[0], got[0])
    tangent_out[...] = tangent
    low_rows = normed[...]
    units = up_own.shape[1]
    block = min(units, 512)

    @pl.when((step == 0) & (pl.program_id(0) == 0))
    def _():
        bias_out[...] = jnp.zeros_like(bias_out)

    for at, (up, down) in enumerate(((up_own, down_own), (up_other, down_other))):
        for first in range(0, units, block):
            own_lanes = slice(first, first + block)
            lanes = slice(at * units + first, at * units + first + block)
            v = mm(low_rows, up[:, own_lanes]) + bias[:, lanes]
            back = mm_nt(tangent, down[own_lanes, :])
            square = v * v
            t = jnp.tanh(v * (root + (root * cubic) * square))
            half = 0.5 * v
            active_out[:, lanes] = (half + half * t).astype(low)
            slope = (0.5 + 0.5 * t) + (half * (1.0 - t * t)) * (
                root + (3.0 * root * cubic) * square
            )
            hidden_back = (back * slope).astype(low)
            back_out[:, lanes] = hidden_back
            bias_out[:, lanes] += jnp.sum(hidden_back.astype(wide), axis=0, keepdims=True)


def feed(core, cotangent, got, normed, ups, bias, downs):
    windows, half, width = got.shape
    units = ups[0].shape[1]
    chunk = math.gcd(half, 256)
    halves = half // chunk
    steps = 2 * halves
    rows = 2 * half * windows
    row = lambda lanes: pl.BlockSpec((chunk, lanes), lambda w, t, core: (w * steps + t, 0))
    out = lambda lanes: jax.ShapeDtypeStruct((rows, lanes), low)
    return pl.pallas_call(
        feed_kernel,
        grid_spec=pltpu.PrefetchScalarGridSpec(
            num_scalar_prefetch=1,
            grid=(windows, steps),
            in_specs=[
                *halves_specs(chunk, width, windows, halves),
                row(width),
                fixed(ups[0]),
                fixed(ups[1]),
                fixed(bias),
                fixed(downs[0]),
                fixed(downs[1]),
            ],
            out_specs=[
                row(width),
                row(2 * units),
                row(2 * units),
                pl.BlockSpec((1, 2 * units), lambda w, t, core: (0, 0)),
            ],
        ),
        out_shape=[
            out(width),
            out(2 * units),
            out(2 * units),
            jax.ShapeDtypeStruct((1, 2 * units), wide),
        ],
        compiler_params=params(48, 2),
        cost_estimate=cost(rows * width * units * 4, rows * units * 8, rows * units * 2),
        name="feed_forward",
    )(core, cotangent, got, normed, *ups, bias, *downs)


def outer_kernel(left, right, own_out, other_out):
    step = pl.program_id(0)
    count = pl.num_programs(0) // 2
    product = mm_tn(left[...], right[...])

    @pl.when(step < count)
    def _():
        other_out[...] = product.astype(low)

    @pl.when(step >= count)
    def _():
        own_out[...] = product


def outer(left, right, name):
    rows, width = left.shape
    lanes = right.shape[1] // 2
    block = min(lanes, 512)
    count = lanes // block
    return pl.pallas_call(
        outer_kernel,
        grid=(2 * count,),
        in_specs=[
            whole(left),
            pl.BlockSpec((rows, block), lambda j: (0, (j + count) % (2 * count))),
        ],
        out_specs=[
            pl.BlockSpec((width, block), lambda j: (0, jnp.maximum(j - count, 0))),
            pl.BlockSpec((width, block), lambda j: (0, jnp.minimum(j, count - 1))),
        ],
        out_shape=[
            jax.ShapeDtypeStruct((width, lanes), wide),
            jax.ShapeDtypeStruct((width, lanes), low),
        ],
        compiler_params=params(40, 1),
        cost_estimate=cost(rows * width * lanes * 2, rows * (lanes * 4 + width * 2)),
        name=name,
    )(left, right)


def backward_kernel(
    tangent, back_hidden, middle_in, decay_in, gate_in, cand_in, up_own, up_other, read_own,
    read_other, gain_two, middle_out, mixed_out, project_out, state_out, gain_out, bias_out,
    states, carry,
):
    step = pl.program_id(1)
    rows, width = tangent.shape
    units = up_own.shape[1]
    channels = read_own.shape[0]

    @pl.when((step == 0) & (pl.program_id(0) == 0))
    def _():
        gain_out[...] = jnp.zeros_like(gain_out)
        bias_out[...] = jnp.zeros_like(bias_out)

    @pl.when(step == 0)
    def _():
        carry[...] = jnp.zeros_like(carry)

    back = mm_nt(back_hidden[:, :units], up_own[...]) + mm_nt(
        back_hidden[:, units:], up_other[...]
    )
    middle = middle_in[...]
    scale = lax.rsqrt(jnp.mean(middle * middle, axis=-1, keepdims=True) + epsilon)
    gain_out[...] += jnp.sum(back * (middle * scale), axis=0, keepdims=True)
    weighted = gain_two[...] * back
    inner = jnp.mean(weighted * middle, axis=-1, keepdims=True)
    back_middle = (
        tangent[...].astype(wide) + scale * weighted - middle * (scale * scale * scale * inner)
    )
    middle_out[...] = back_middle
    mixed = back_middle.astype(low)
    mixed_out[...] = mixed
    states[:, :channels] = mm_nt(mixed, read_own[...])
    states[:, channels:] = mm_nt(mixed, read_other[...])

    group = min(channels, 256)
    place = rows_of(8, group)
    count = rows // 16

    def sweep(index, _):
        base = pl.multiple_of((count - 1 - index) * 16, 16)
        for at in (0, 1):
            for lane in range(0, channels, group):
                lanes = slice(at * channels + lane, at * channels + lane + group)
                later = carry[:, lanes]
                kept = []
                for sub in (8, 0):
                    d = decay_in[pl.ds(base + sub, 8), lanes]
                    s = states[pl.ds(base + sub, 8), lanes]
                    a = d
                    b = d * s
                    for hop in (1, 2, 4):
                        inside = place < 8 - hop
                        a_next = jnp.where(inside, pltpu.roll(a, 8 - hop, 0), 1.0)
                        b_next = jnp.where(inside, pltpu.roll(b, 8 - hop, 0), 0.0)
                        b = a * b_next + b
                        a = a * a_next
                    u = a * later + b
                    carried = s + jnp.where(place < 7, pltpu.roll(u, 7, 0), later)
                    later = jnp.broadcast_to(u[0:1, :], u.shape)
                    kept.insert(0, carried)
                carry[:, lanes] = later
                both = jnp.concatenate(kept, axis=0)
                gate = (both * gate_in[pl.ds(base, 16), lanes].astype(wide)).astype(low)
                cand = (both * cand_in[pl.ds(base, 16), lanes].astype(wide)).astype(low)
                first = 2 * at * channels + lane
                project_out[pl.ds(base, 16), first : first + group] = gate
                project_out[pl.ds(base, 16), first + channels : first + channels + group] = cand
                rounded = gate.astype(wide)
                bias_out[:, lanes] += rounded[:8] + rounded[8:]
        return 0

    lax.fori_loop(0, count, sweep, 0)

    @pl.when(step == pl.num_programs(1) - 1)
    def _():
        state_out[0] = carry[0:1, :]


def backward(windows, tangent, back_hidden, middle, decay, gate, cand, ups, reads, gain_two):
    rows, width = tangent.shape
    units = ups[0].shape[1]
    channels = reads[0].shape[0]
    length = rows // windows
    chunk = math.gcd(length, 256)
    steps = length // chunk
    row = lambda lanes: pl.BlockSpec((chunk, lanes), lambda w, t: (w * steps + steps - 1 - t, 0))
    out = lambda lanes, dtype: jax.ShapeDtypeStruct((rows, lanes), dtype)
    return pl.pallas_call(
        backward_kernel,
        grid=(windows, steps),
        in_specs=[
            row(width),
            row(2 * units),
            row(width),
            row(2 * channels),
            row(2 * channels),
            row(2 * channels),
            whole(ups[0]),
            whole(ups[1]),
            whole(reads[0]),
            whole(reads[1]),
            whole(gain_two),
        ],
        out_specs=[
            row(width),
            row(width),
            row(4 * channels),
            pl.BlockSpec((1, 1, 2 * channels), lambda w, t: (w, 0, 0)),
            pl.BlockSpec((1, width), lambda w, t: (0, 0)),
            pl.BlockSpec((8, 2 * channels), lambda w, t: (0, 0)),
        ],
        out_shape=[
            out(width, wide),
            out(width, low),
            out(4 * channels, low),
            jax.ShapeDtypeStruct((windows, 1, 2 * channels), wide),
            jax.ShapeDtypeStruct((1, width), wide),
            jax.ShapeDtypeStruct((8, 2 * channels), wide),
        ],
        scratch_shapes=[
            pltpu.VMEM((chunk, 2 * channels), wide),
            pltpu.VMEM((8, 2 * channels), wide),
        ],
        compiler_params=params(48, 2),
        cost_estimate=cost(
            rows * width * (2 * units + 2 * channels), rows * (units * 4 + channels * 24)
        ),
        name="backward_mixer",
    )(tangent, back_hidden, middle, decay, gate, cand, *ups, *reads, gain_two)


def entry_kernel(
    core, own, got, project, middle_in, mixer_own, mixer_other, gain, taps,
    grad_out, gain_out, taps_out, rim,
):
    step = pl.program_id(1)
    steps = pl.num_programs(1)
    half_chunks = steps // 2
    position = steps - 1 - step
    rows, width = own.shape[1:]
    tap_count = taps.shape[0]
    lanes = mixer_own.shape[1]

    @pl.when((step == 0) & (pl.program_id(0) == 0))
    def _():
        gain_out[...] = jnp.zeros_like(gain_out)
        taps_out[...] = jnp.zeros_like(taps_out)

    @pl.when(step == 0)
    def _():
        rim[rows : rows + 8, :] = jnp.zeros((8, width), wide)

    rim[0:rows, :] = mm_nt(project[:, :lanes], mixer_own[...]) + mm_nt(
        project[:, lanes:], mixer_other[...]
    )
    x = jnp.where(position // half_chunks == core[0], own[0], got[0]).astype(wide)
    scale = lax.rsqrt(jnp.mean(x * x, axis=-1, keepdims=True) + epsilon)
    unit = x * scale
    normed = unit * gain[...]
    back = jnp.zeros((rows, width), wide)
    for tap in range(tap_count):
        ahead = rim[tap_count - 1 - tap : tap_count - 1 - tap + rows, :]
        back = back + taps[tap : tap + 1, :] * ahead
        taps_out[tap : tap + 1, :] += jnp.sum(ahead * normed, axis=0, keepdims=True)
    rim[rows : rows + 8, :] = rim[0:8, :]
    gain_out[...] += jnp.sum(back * unit, axis=0, keepdims=True)
    weighted = gain[...] * back
    inner = jnp.mean(weighted * x, axis=-1, keepdims=True)
    grad_out[...] = (
        middle_in[...] + scale * weighted - x * (scale * scale * scale * inner)
    ).astype(low)


def entry(core, inputs, got, project, back_middle, mixers, gain, taps):
    windows, half, width = got.shape
    chunk = math.gcd(half, 256)
    halves = half // chunk
    steps = 2 * halves
    rows = 2 * half * windows
    row = lambda lanes: pl.BlockSpec(
        (chunk, lanes), lambda w, t, core: (w * steps + steps - 1 - t, 0)
    )
    return pl.pallas_call(
        entry_kernel,
        grid_spec=pltpu.PrefetchScalarGridSpec(
            num_scalar_prefetch=1,
            grid=(windows, steps),
            in_specs=[
                pl.BlockSpec(
                    (1, chunk, width),
                    lambda w, t, core: (windows * core[0] + w, (steps - 1 - t) % halves, 0),
                ),
                pl.BlockSpec((1, chunk, width), lambda w, t, core: (w, (steps - 1 - t) % halves, 0)),
                row(project.shape[1]),
                row(width),
                fixed(mixers[0]),
                fixed(mixers[1]),
                fixed(gain),
                fixed(taps),
            ],
            out_specs=[
                row(width),
                pl.BlockSpec((1, width), lambda w, t, core: (0, 0)),
                pl.BlockSpec(taps.shape, lambda w, t, core: (0, 0)),
            ],
            scratch_shapes=[pltpu.VMEM((chunk + 8, width), wide)],
        ),
        out_shape=[
            jax.ShapeDtypeStruct((rows, width), low),
            jax.ShapeDtypeStruct((1, width), wide),
            jax.ShapeDtypeStruct(taps.shape, wide),
        ],
        compiler_params=params(48, 2),
        cost_estimate=cost(rows * width * project.shape[1], rows * project.shape[1] * 4),
        name="input_gradient",
    )(core, inputs, got, project, back_middle, *mixers, gain, taps)


def exit_kernel(active, middle, down_own, down_other, out):
    units = down_own.shape[0]
    out[...] = (
        middle[...] + mm(active[:, :units], down_own[...]) + mm(active[:, units:], down_other[...])
    ).astype(low)


def leave(active, middle, downs):
    rows, width = middle.shape
    chunk = math.gcd(rows, 512)
    row = lambda lanes: pl.BlockSpec((chunk, lanes), lambda t: (t, 0))
    return pl.pallas_call(
        exit_kernel,
        grid=(rows // chunk,),
        in_specs=[row(active.shape[1]), row(width), whole(downs[0]), whole(downs[1])],
        out_specs=row(width),
        out_shape=jax.ShapeDtypeStruct((rows, width), low),
        compiler_params=params(48, 1),
        cost_estimate=cost(rows * width * active.shape[1], rows * active.shape[1] * 3),
        name="block_output",
    )(active, middle, *downs)


def partner(array):
    return lax.ppermute(array, "tensor", [(0, 1), (1, 0)])


def across(array, bits):
    sizes = (lax.axis_size("dp"), lax.axis_size("tensor"))
    route = [
        (d * sizes[1] + c, (d ^ (1 << bits[c])) * sizes[1] + c)
        for d in range(sizes[0])
        for c in range(sizes[1])
    ]
    return lax.ppermute(array, ("dp", "tensor"), route)


def bit_orders():
    count = lax.axis_size("dp").bit_length() - 1
    first = list(range(count))
    second = first[:]
    if count >= 3:
        second[:3] = [2, 0, 1]
    return list(zip(first, second))


def sum_over_dp(total):
    index, core = lax.axis_index("dp"), lax.axis_index("tensor")
    stages = []
    for bits in bit_orders():
        bit = jnp.where(core == 0, (index >> bits[0]) & 1, (index >> bits[1]) & 1)
        half = total.shape[0] // 2
        keep = lax.dynamic_slice_in_dim(total, bit * half, half)
        send = lax.dynamic_slice_in_dim(total, (1 - bit) * half, half).astype(low)
        total = keep + across(send, bits).astype(wide)
        stages.append((bits, bit))
    piece = total.astype(low)
    for bits, bit in reversed(stages):
        other = across(piece, bits)
        piece = jnp.where(
            bit == 0, jnp.concatenate([piece, other]), jnp.concatenate([other, piece])
        )
    return piece


def sum_small(values):
    for bit in range(lax.axis_size("dp").bit_length() - 1):
        values = values + across(values, (bit, bit))
    return values


def local(
    inputs,
    initial_state,
    first_gain,
    causal_filter,
    mixer_weight,
    gate_bias,
    readout_weight,
    second_gain,
    up_weight,
    up_bias,
    down_weight,
    cotangent,
):
    sides = lax.axis_size("tensor")
    windows = inputs.shape[0] // sides
    half, width = inputs.shape[1:]
    channels = gate_bias.shape[0]
    units = up_bias.shape[0]
    core = lax.axis_index("tensor")
    core_at = core.reshape(1).astype(jnp.int32)

    def own_windows(array):
        return lax.dynamic_slice_in_dim(array, core * windows, windows)

    def other_windows(array):
        return lax.dynamic_slice_in_dim(array, (1 - core) * windows, windows)

    mixer = mixer_weight.reshape(width, 2 * channels)
    got_inputs = partner(other_windows(inputs))
    short = jnp.concatenate([gate_bias[None], up_bias.reshape(-1, channels), other_windows(initial_state)])
    got_short = partner(short)
    bias_rows = 1 + units // channels
    mixers = (mixer, partner(mixer))
    reads = (readout_weight, partner(readout_weight))
    got_cotangent = partner(other_windows(cotangent))
    ups = (up_weight, partner(up_weight))
    downs = (down_weight, partner(down_weight))
    gate_bias_all = jnp.concatenate([gate_bias, got_short[0]])[None]
    up_bias_all = jnp.concatenate([up_bias, got_short[1:bias_rows].reshape(-1)])[None]
    start = jnp.concatenate([own_windows(initial_state), got_short[bias_rows:]], axis=1)[:, None]
    gain, gain_two = first_gain[None], second_gain[None]

    filtered, decay, gate, cand, states, middle, normed = forward(
        core_at, inputs, got_inputs, gain, causal_filter, mixers, gate_bias_all, start, reads, gain_two
    )
    tangent, active, back_hidden, up_bias_grad = feed(
        core_at, cotangent, got_cotangent, normed, ups, up_bias_all, downs
    )
    down_own, down_other = outer(tangent, active, "down_gradient")
    up_own, up_other = outer(normed, back_hidden, "up_gradient")
    feed_total = jnp.concatenate([down_own, up_own]) + partner(
        jnp.concatenate([down_other, up_other])
    ).astype(wide)
    feed_sum = sum_over_dp(feed_total)
    back_middle, back_mixed, project, state_grad, gain_two_grad, gate_bias_grad = backward(
        windows, tangent, back_hidden, middle, decay, gate, cand, ups, reads, gain_two
    )
    read_own, read_other = outer(back_mixed, states, "readout_gradient")
    mixer_own, mixer_other = outer(filtered, project, "mixer_gradient")
    mixer_total = jnp.concatenate([mixer_own, read_own], axis=1) + partner(
        jnp.concatenate([mixer_other, read_other], axis=1)
    ).astype(wide)
    mixer_sum = sum_over_dp(mixer_total)
    input_grad, gain_grad, taps_grad = entry(
        core_at, inputs, got_inputs, project, back_middle, mixers, gain, causal_filter
    )
    output = leave(active, middle, downs)

    gate_bias_grad = jnp.sum(gate_bias_grad, axis=0)
    up_bias_grad = up_bias_grad[0]
    common = jnp.concatenate([gain_grad[0], taps_grad.reshape(-1), gain_two_grad[0]])
    sent = partner(jnp.concatenate([common, gate_bias_grad[channels:], up_bias_grad[units:]]))
    short_sum = sum_small(
        jnp.concatenate([common, gate_bias_grad[:channels], up_bias_grad[:units]]) + sent
    )
    cuts = [width, width + causal_filter.size, 2 * width + causal_filter.size]
    cuts += [cuts[-1] + channels]
    gain_sum, taps_sum, gain_two_sum, gate_bias_sum, up_bias_sum = jnp.split(short_sum, cuts)

    def place(mine, got):
        return jnp.where(core == 0, jnp.concatenate([mine, got]), jnp.concatenate([got, mine]))

    def give_back(rows):
        parts = rows.reshape(windows, sides, half, width)
        mine = lax.dynamic_index_in_dim(parts, core, 1, keepdims=False)
        other = lax.dynamic_index_in_dim(parts, 1 - core, 1, keepdims=False)
        return place(mine, partner(other))

    state_rows = state_grad[:, 0]
    state_gradient = place(state_rows[:, :channels], partner(state_rows[:, channels:]))
    return (
        give_back(output),
        give_back(input_grad),
        state_gradient,
        gain_sum,
        taps_sum.reshape(causal_filter.shape),
        mixer_sum[:, : 2 * channels].astype(wide).reshape(width, 2, channels),
        gate_bias_sum,
        mixer_sum[:, 2 * channels :].astype(wide).T,
        gain_two_sum,
        feed_sum[width:].astype(wide),
        up_bias_sum,
        feed_sum[:width].astype(wide).T,
    )


def solution(mesh):
    return jax.shard_map(
        local,
        mesh=mesh,
        in_specs=(
            P("dp", "tensor", None),
            P("dp", "tensor"),
            P(),
            P(),
            P(None, None, "tensor"),
            P("tensor"),
            P("tensor", None),
            P(),
            P(None, "tensor"),
            P("tensor"),
            P("tensor", None),
            P("dp", "tensor", None),
        ),
        out_specs=(
            P("dp", "tensor", None),
            P("dp", "tensor", None),
            P("dp", "tensor"),
            P(),
            P(),
            P(None, None, "tensor"),
            P("tensor"),
            P("tensor", None),
            P(),
            P(None, "tensor"),
            P("tensor"),
            P("tensor", None),
        ),
        check_vma=False,
    )
```

time: 897 us -> 266 us (0.30)
  local copies, waits for them, and re-layouts: 264 us -> 28.6 us
  other arithmetic: 202 us -> 30.5 us
  waiting for transfers between devices: 204 us -> 40.5 us
  Pallas kernels: 0 us -> 129 us
  matrix products: 114 us -> 0 us
  blocking collectives: 85.4 us -> 0 us
  starting transfers between devices: 5.03 us -> 35.4 us
  between operations: 15.8 us -> 1.33 us
    slice x99 -> x3, local copies, waits for them, and re-layouts: 147 us -> 0.01 us  [the longest x1 0.01 us: local(): gate_bias_all = jnp.concatenate([gate_bias, got_short[0]])[None]]
    psum x1 -> x0, waiting for transfers between devices: 142 us -> none  [local(): lax.psum((mixer_gradient, gate_bias_gradient, readout_gradient, up_gradie...]
    pallas_call x0 -> x9, Pallas kernels: none -> 129 us  [the longest x1 34.6 us: forward(): pl.pallas_call(forward_kernel, grid_spec=pltpu.PrefetchScalarGridSpec(num...]
    dot_general x12 -> x0, matrix products: 114 us -> none  [the longest x4 43 us: contract(): lax.dot_general(left, right, (((left_dim,), (right_dim,)), ((), ())), pre...]
    psum x2 -> x0, blocking collectives: 85.4 us -> none  [the longest x1 44.7 us: local(): lax.psum((mixer_gradient, gate_bias_gradient, readout_gradient, up_gradie...]
    unnamed x174 -> x75, local copies, waits for them, and re-layouts: 56.5 us -> 16.8 us
    ppermute x2 -> x33, waiting for transfers between devices: 0.77 us -> 40.5 us  [the longest x20 40.4 us: across(): return lax.ppermute(array, ('dp', 'tensor'), route)]
    mul x22 -> x0, other arithmetic: 35.1 us -> none  [the longest x2 12.8 us: chain_scan(): running_factor = factor_blocks[:, position] * running_factor]
  transfers between devices with their start and end apart: 11 -> 33, of which waited for: 6 -> 11; matrix products, arithmetic and copies ran while one was open for 16% -> 14% of each run, Pallas kernels for 0% -> 25%
where the time goes in v1:
time: 266 us; the launch traced here: 265 us
  Pallas kernels  129 us (48%)
  waiting for transfers between devices  40.5 us (15%)
  starting transfers between devices  35.4 us (13%)
  other arithmetic  30.5 us (11%)
  local copies, waits for them, and re-layouts  28.6 us (11%)
    ppermute x20, waiting for transfers between devices, across(): return lax.ppermute(array, ('dp', 'tensor'), route)  40.4 us
    pallas_call x1, Pallas kernels, forward(): pl.pallas_call(forward_kernel, grid_spec=pltpu.PrefetchScalarGridSpec(num...  34.6 us
    ppermute x20, starting transfers between devices, across(): return lax.ppermute(array, ('dp', 'tensor'), route)  31.2 us
    pallas_call x1, Pallas kernels, backward(): pl.pallas_call(backward_kernel, grid=(windows, steps), in_specs=[row(widt...  25.9 us
    pallas_call x4, Pallas kernels, outer(): pl.pallas_call(outer_kernel, grid=(2 * count,), in_specs=[whole(left), pl...  22.1 us
    pallas_call x1, Pallas kernels, feed(): pl.pallas_call(feed_kernel, grid_spec=pltpu.PrefetchScalarGridSpec(num_sc...  21 us
    pallas_call x1, Pallas kernels, entry(): pl.pallas_call(entry_kernel, grid_spec=pltpu.PrefetchScalarGridSpec(num_s...  17.9 us
    unnamed x75, local copies, waits for them, and re-layouts  16.8 us
  transfers between devices with their start and end apart: 33, of which 11 were waited for; matrix products, arithmetic and copies ran while one was open for 14% of the time, Pallas kernels for 25%

profile of v1, /device:TPU:0, one launch (start us, length us, event | category | flops | bytes accessed | tf_op | source)
XLA Modules:
  0.0 265.4 jit_solution(6546369791884522752)
XLA Ops:
  1.2 2.4 constant_dynamic-slice_fusion.2
  4.6 2.3 constant_dynamic-slice_fusion.3
  8.0 1.0 copy-done.17
  9.0 34.6 %forward_mixer.1 = (bf16[2048,512]{1,0:T(8,128)(2,1)}, f32[2048,1024]{1,0:T(8,128)}, bf16[2048,1024]{1,0:T(8,128)(2,1)}, bf16[2048,1024]{1,0:T(8,128)(2,1)}, bf1...) custom-call(s32[1]{0:T(128)} %bitcast.core, bf16[4,512,512]{2,1,0:T(8,128)(2,1)} %own.5, ...), custom_call_target="tpu_custom_call" | custom-call | flops 6442450944 | bytes 25165824 | tf_op jit(solution)/shard_map/forward_mixer/pallas_call | solution.py:157
  43.7 21.0 %feed_forward.1 = (bf16[2048,512]{1,0:T(8,128)(2,1)}, bf16[2048,2048]{1,0:T(8,128)(2,1)}, bf16[2048,2048]{1,0:T(8,128)(2,1)}, f32[1,2048]{1,0:T(1,128)S(1)}) custom-call(s32[1]{0:T(128)} %bitcast.core, bf16[4,512,512]{2,1,0:T(8,128)(2,1)} %own.4, bf16[2,512,512]{2,1,0:T(8,128)(2,1)} %collective-permute-done.got, ...), custom_call_target="tpu_custom_call" | custom-call | flops 8589934592 | bytes 16777216 | tf_op jit(solution)/shard_map/feed_forward/pallas_call | solution.py:248
  64.7 3.4 %copy-done = bf16[2048,2048]{1,0:T(8,128)(2,1)S(1)} copy-done((bf16[2048,2048]{1,0:T(8,128)(2,1)S(1)}, bf16[2048,2048]{1,0:T(8,128)(2,1)}, u32[]{:S(2)}) %copy-start) | copy-done | bytes 8388632
  68.1 6.4 %up_gradient.1 = (f32[512,1024]{1,0:T(8,128)S(1)}, bf16[512,1024]{1,0:T(8,128)(2,1)S(1)}) custom-call(bf16[2048,512]{1,0:T(8,128)(2,1)S(1)} %copy-done.24, bf16[2048,2048]{1,0:T(8,128)(2,1)S(1)} %copy-done), custom_call_target="tpu_custom_call" | custom-call | flops 4294967296 | bytes 10485760 | tf_op jit(solution)/shard_map/up_gradient/pallas_call | solution.py:300
  74.5 1.3 copy-done.2
  75.8 25.9 %backward_mixer.1 = (f32[2048,512]{1,0:T(8,128)}, bf16[2048,512]{1,0:T(8,128)(2,1)S(1)}, bf16[2048,2048]{1,0:T(8,128)(2,1)}, f32[2,1,1024]{2,1,0:T(1,128)S(1)}, ...) custom-call(bf16[2048,512]{1,0:T(8,128)(2,1)} %get-tuple-element.43.tangent.left, ...), custom_call_target="tpu_custom_call" | custom-call | flops 6442450944 | bytes 33554432 | tf_op jit(solution)/shard_map/backward_mixer/pallas_call | solution.py:410
  101.7 3.0 %readout_gradient.1 = (f32[512,512]{1,0:T(8,128)S(1)}, bf16[512,512]{1,0:T(8,128)(2,1)S(1)}) custom-call(bf16[2048,512]{1,0:T(8,128)(2,1)S(1)} %get-tuple-element.59.left, bf16[2048,1024]{1,0:T(8,128)(2,1)S(1)} %copy-done.22), custom_call_target="tpu_custom_call" | custom-call | flops 2147483648 | bytes 6291456 | tf_op jit(solution)/shard_map/readout_gradient/pallas_call | solution.py:300
  104.7 1.0 copy-done.16
  105.7 3.4 %copy-done.1 = bf16[2048,2048]{1,0:T(8,128)(2,1)S(1)} copy-done((bf16[2048,2048]{1,0:T(8,128)(2,1)S(1)}, bf16[2048,2048]{1,0:T(8,128)(2,1)}, u32[]{:S(2)}) %copy-start.1) | copy-done | bytes 8388632
  109.1 6.4 %mixer_gradient.1 = (f32[512,1024]{1,0:T(8,128)S(1)}, bf16[512,1024]{1,0:T(8,128)(2,1)S(1)}) custom-call(bf16[2048,512]{1,0:T(8,128)(2,1)S(1)} %copy-done.23, bf16[2048,2048]{1,0:T(8,128)(2,1)S(1)} %copy-done.1), custom_call_target="tpu_custom_call" | custom-call | flops 4294967296 | bytes 10485760 | tf_op jit(solution)/shard_map/mixer_gradient/pallas_call | solution.py:300
  115.5 1.3 pad_maximum_fusion.1
  116.9 1.5 copy-done.6
  118.4 6.4 %down_gradient.1 = (f32[512,1024]{1,0:T(8,128)S(1)}, bf16[512,1024]{1,0:T(8,128)(2,1)S(1)}) custom-call(bf16[2048,512]{1,0:T(8,128)(2,1)S(1)} %copy-done.6, bf16[2048,2048]{1,0:T(8,128)(2,1)S(1)} %bitcast.36), custom_call_target="tpu_custom_call" | custom-call | flops 4294967296 | bytes 10485760 | tf_op jit(solution)/shard_map/down_gradient/pallas_call | solution.py:300
  124.8 1.6 pad_maximum_fusion
  126.9 17.9 %input_gradient.1 = (bf16[2048,512]{1,0:T(8,128)(2,1)S(1)}, f32[1,512]{1,0:T(1,128)S(1)}, f32[4,512]{1,0:T(4,128)S(1)}) custom-call(s32[1]{0:T(128)} %bitcast.core, bf16[4,512,512]{2,1,0:T(8,128)(2,1)} %own.5, bf16[2,512,512]{2,1,0:T(8,128)(2,1)} %collective-permute-done.1.got, bf16[2048,2048]{1,0:T(8,128)(2,1)} %get-tuple-element.48.project.right, ...), custom_call_target="tpu_custom_call" | custom-call | flops 4294967296 | bytes 16777216 | tf_op jit(solution)/shard_map/input_gradient/pallas_call | solution.py:505
  144.8 1.3 copy-done.7
  146.8 2.4 maximum_add_fusion.1
  149.3 2.9 %collective-permute-start.16 = (bf16[256,1536]{1,0:T(8,128)(2,1)S(1)}, bf16[256,1536]{1,0:T(8,128)(2,1)S(1)}, u32[]{:S(2)}, u32[]{:S(2)}) collective-permute-start(bf16[256,1536]{1,0:T(8,128)(2,1)S(1)} %dynamic-slice_convert_fusion.1), channel_id=1, source_target_pairs={{0,2},{1,9},{2,0},{3,11},{4,6},{5,13},{6,4},{7,15},{8,10},{9,1},{1... | collective-permute-start | bytes 2359304 | tf_op jit(solution)/shard_map/ppermute | solution.py:575
  152.4 1.2 collective-permute-start.8
  153.6 8.9 %collective-permute-done.11 = f32[4608]{0:T(1024)S(1)} collective-permute-done((f32[4608]{0:T(1024)S(1)}, f32[4608]{0:T(1024)S(1)}, u32[]{:S(2)}, u32[]{:S(2)}) %collective-permute-start.11) | collective-permute-done | bytes 18464 | tf_op jit(solution)/shard_map/ppermute | solution.py:575
  162.5 2.0 collective-permute-start.12
  164.6 2.4 maximum_add_fusion
  167.1 1.6 collective-permute-start.25
  169.6 7.6 %block_output.1 = bf16[2048,512]{1,0:T(8,128)(2,1)S(1)} custom-call(bf16[2048,2048]{1,0:T(8,128)(2,1)} %get-tuple-element.41.active.right, f32[2048,512]{1,0:T(8,128)} %get-tuple-element.42.middle.middle_in, bf16[1024,512]{1,0:T(8,128)(2,1)S(1)} %copy-done.13, bf16[1024,512]{1,0:T(8,128)(2,1)S(1)} %copy-done.15), custom_call_target="tpu_custom_call" | custom-call | flops 4294967296 | bytes 12582912 | tf_op jit(solution)/shard_map/block_output/pallas_call | solution.py:552
  177.9 1.4 collective-permute-start.13
  179.4 0.7 collective-permute-start.18
  180.2 4.8 %collective-permute-done.25 = bf16[512,1024]{1,0:T(8,128)(2,1)} collective-permute-done((bf16[512,1024]{1,0:T(8,128)(2,1)S(1)}, bf16[512,1024]{1,0:T(8,128)(2,1)}, u32[]{:S(2)}, u32[]{:S(2)}) %collective-permute-start.25) | collective-permute-done | bytes 1048608 | tf_op jit(solution)/shard_map/ppermute | solution.py:575
  185.0 1.7 convert_add_fusion
  186.9 3.2 %collective-permute-start.19 = (bf16[32,1536]{1,0:T(8,128)(2,1)S(1)}, bf16[32,1536]{1,0:T(8,128)(2,1)S(1)}, u32[]{:S(2)}, u32[]{:S(2)}) collective-permute-start(bf16[32,1536]{1,0:T(8,128)(2,1)S(1)} %dynamic-slice_convert_fusion.7), channel_id=1, source_target_pairs={{0,16},{1,17},{2,18},{3,19},{4,20},{5,21},{6,22},{7,23},{8,24},{9,... | collective-permute-start | bytes 294920 | tf_op jit(solution)/shard_map/ppermute | solution.py:575
  190.1 8.7 %collective-permute-done.26 = bf16[256,1024]{1,0:T(8,128)(2,1)S(1)} collective-permute-done((bf16[256,1024]{1,0:T(8,128)(2,1)S(1)}, bf16[256,1024]{1,0:T(8,128)(2,1)S(1)}, u32[]{:S(2)}, u32[]{:S(2)}) %collective-permute-start.26) | collective-permute-done | bytes 524320 | tf_op jit(solution)/shard_map/ppermute | solution.py:575
  199.0 1.4 collective-permute-start.27
  200.4 3.0 %collective-permute-start.20 = (bf16[32,1536]{1,0:T(8,128)(2,1)S(1)}, bf16[32,1536]{1,0:T(8,128)(2,1)S(1)}, u32[]{:S(2)}, u32[]{:S(2)}) collective-permute-start(bf16[32,1536]{1,0:T(8,128)(2,1)S(1)} %add_convert_fusion.1), channel_id=1, source_target_pairs={{0,16},{1,17},{2,18},{3,19},{4,20},{5,21},{6,22},{7,23},{8,24},{9,... | collective-permute-start | bytes 294920 | tf_op jit(solution)/shard_map/ppermute | solution.py:575
  203.5 3.1 %collective-permute-done.27 = bf16[128,1024]{1,0:T(8,128)(2,1)S(1)} collective-permute-done((bf16[128,1024]{1,0:T(8,128)(2,1)S(1)}, bf16[128,1024]{1,0:T(8,128)(2,1)S(1)}, u32[]{:S(2)}, u32[]{:S(2)}) %collective-permute-start.27) | collective-permute-done | bytes 262176 | tf_op jit(solution)/shard_map/ppermute | solution.py:575
  206.7 2.9 %collective-permute-start.28 = (bf16[64,1024]{1,0:T(8,128)(2,1)S(1)}, bf16[64,1024]{1,0:T(8,128)(2,1)S(1)}, u32[]{:S(2)}, u32[]{:S(2)}) collective-permute-start(bf16[64,1024]{1,0:T(8,128)(2,1)S(1)} %dynamic-slice_convert_fusion.6), channel_id=1, source_target_pairs={{0,16},{1,17},{2,18},{3,19},{4,20},{5,21},{6,22},{7,23},{8,24},{9,... | collective-permute-start | bytes 393224 | tf_op jit(solution)/shard_map/ppermute | solution.py:575
  209.6 1.4 collective-permute-start.21
  211.0 3.1 %collective-permute-done.28 = bf16[64,1024]{1,0:T(8,128)(2,1)S(1)} collective-permute-done((bf16[64,1024]{1,0:T(8,128)(2,1)S(1)}, bf16[64,1024]{1,0:T(8,128)(2,1)S(1)}, u32[]{:S(2)}, u32[]{:S(2)}) %collective-permute-start.28) | collective-permute-done | bytes 131104 | tf_op jit(solution)/shard_map/ppermute | solution.py:575
  214.2 1.5 collective-permute-start.29
  216.0 0.9 collective-permute-start.22
  216.9 4.6 %collective-permute-done.29 = bf16[64,1024]{1,0:T(8,128)(2,1)S(1)} collective-permute-done((bf16[64,1024]{1,0:T(8,128)(2,1)S(1)}, bf16[64,1024]{1,0:T(8,128)(2,1)S(1)}, u32[]{:S(2)}, u32[]{:S(2)}) %collective-permute-start.29) | collective-permute-done | bytes 131104 | tf_op jit(solution)/shard_map/ppermute | solution.py:575
  221.5 0.8 maximum_select_fusion.8
  222.2 1.2 dynamic-slice_bitcast_fusion.3
  223.4 3.0 %collective-permute-start.14 = (f32[4608]{0:T(1024)S(1)}, f32[4608]{0:T(1024)S(1)}, u32[]{:S(2)}, u32[]{:S(2)}) collective-permute-start(f32[4608]{0:T(1024)S(1)} %add.118), channel_id=1, source_target_pairs={{0,16},{1,17},{2,18},{3,19},{4,20},{5,21},{6,22},{7,23},{8,24},{9,... | collective-permute-start | bytes 55304 | tf_op jit(solution)/shard_map/ppermute | solution.py:575
  227.0 1.3 collective-permute-done.14
  229.5 1.4 maximum_select_fusion.6
  231.6 1.3 maximum_select_fusion.5
  232.9 1.7 collective-permute-start.23
  234.6 1.3 fusion
  235.9 3.2 %maximum_select_fusion.1 = bf16[4,512,512]{2,1,0:T(8,128)(2,1)} fusion(bf16[2,512,512]{2,1,0:T(8,128)(2,1)} %collective-permute-done.8, bf16[2,512,512]{2,1,0:T(8,128)(2,1)S(1)} %get-tuple-element.82, pred[]{:T(512)S(6)} %eq.10), kind=kLoop, calls=%fused_computation.3 | loop fusion | flops 3145728 | bytes 4194305 | tf_op jit(solution)/shard_map/jit(_where)/select_n | solution.py:693
  239.1 1.1 collective-permute-done.31
  240.7 2.3 collective-permute-start.32
  243.0 3.2 %maximum_select_fusion = bf16[4,512,512]{2,1,0:T(8,128)(2,1)} fusion(bf16[2,512,512]{2,1,0:T(8,128)(2,1)} %collective-permute-done.7, bf16[2,512,512]{2,1,0:T(8,128)(2,1)S(1)} %get-tuple-element.84, pred[]{:T(512)S(6)} %eq.10), kind=kLoop, calls=%fused_computation.2 | loop fusion | flops 3145728 | bytes 4194305 | tf_op jit(solution)/shard_map/jit(_where)/select_n | solution.py:693
  246.2 1.7 collective-permute-done.23
  247.9 1.8 maximum_select_fusion.3
  249.7 1.2 convert_bitcast_fusion.1
  250.9 1.3 copy.24
  252.2 1.5 slice_convert_fusion.1
  253.7 2.8 %reshape.72 = f32[512,2,512]{2,1,0:T(2,128)} reshape(f32[512,1024]{1,0:T(8,128)S(1)} %slice_convert_fusion.1) | data formatting | bytes 4194304 | tf_op jit(solution)/shard_map/reshape | solution.py:709
  256.4 2.8 %collective-permute-done.32 = bf16[512,1024]{1,0:T(8,128)(2,1)} collective-permute-done((bf16[512,1024]{1,0:T(8,128)(2,1)S(1)}, bf16[512,1024]{1,0:T(8,128)(2,1)}, u32[]{:S(2)}, u32[]{:S(2)}) %collective-permute-start.32) | collective-permute-done | bytes 1048608 | tf_op jit(solution)/shard_map/ppermute | solution.py:575
  259.3 2.5 maximum_select_fusion.2
  261.8 1.8 convert_bitcast_fusion
  263.6 1.8 copy.25
  (150 shorter events, 10.1 us)
Async XLA Ops:
  0.6 6.8 %collective-permute-start.4 = (bf16[512,512]{1,0:T(8,128)(2,1)}, bf16[512,512]{1,0:T(8,128)(2,1)}, u32[]{:S(2)}, u32[]{:S(2)}) collective-permute-start(bf16[512,512]{1,0:T(8,128)(2,1)} %read_own.3), channel_id=1, source_target_pairs={{0,1},{1,0},{2,3},{3,2},{4,5},{5,4},{6,7},{7,6},{8,9},{9,8},{10,11... | collective-permute-start | bytes 1572872 | tf_op jit(solution)/shard_map/ppermute | solution.py:565
  1.2 2.4 copy-start.25
  1.2 3.2 %copy-start.27 = (f32[1024]{0:T(1024)S(1)}, f32[1024]{0:T(1024)}, u32[]{:S(2)}) copy-start(f32[1024]{0:T(1024)} %param.21) | copy-start | bytes 12292
  1.2 3.2 %copy-start.28 = (f32[4,512]{1,0:T(4,128)S(1)}, f32[4,512]{1,0:T(4,128)}, u32[]{:S(2)}) copy-start(f32[4,512]{1,0:T(4,128)} %param.13) | copy-start | bytes 24580
  1.2 3.3 %copy-start.29 = (f32[512]{0:T(512)S(1)}, f32[512]{0:T(512)}, u32[]{:S(2)}) copy-start(f32[512]{0:T(512)} %param.17) | copy-start | bytes 6148
  3.5 4.4 %collective-permute-start.1 = (bf16[2,512,512]{2,1,0:T(8,128)(2,1)}, bf16[2,512,512]{2,1,0:T(8,128)(2,1)}, u32[]{:S(2)}, u32[]{:S(2)}) collective-permute-start(bf16[2,512,512]{2,1,0:T(8,128)(2,1)} %constant_dynamic-slice_fusion.2), channel_id=1, source_target_pairs={{0,1},{1,0},{2,3},{3,2},{4,5},{5,4},{6,7},{7,6},{8,9},{9,8},{10,11... | collective-permute-start | bytes 3145736 | tf_op jit(solution)/shard_map/ppermute | solution.py:565
  3.6 3.7 %copy-start.11 = (bf16[512,1024]{1,0:T(8,128)(2,1)S(1)}, bf16[512,1024]{1,0:T(8,128)(2,1)}, u32[]{:S(2)}) copy-start(bf16[512,1024]{1,0:T(8,128)(2,1)} %up_own.3) | copy-start | bytes 3145732
  3.6 3.8 %copy-start.12 = (bf16[1024,512]{1,0:T(8,128)(2,1)S(1)}, bf16[1024,512]{1,0:T(8,128)(2,1)}, u32[]{:S(2)}) copy-start(bf16[1024,512]{1,0:T(8,128)(2,1)} %down_own.3) | copy-start | bytes 3145732
  3.6 4.4 %copy-start.19 = (f32[4,512]{1,0:T(4,128)S(1)}, f32[4,512]{1,0:T(4,128)}, u32[]{:S(2)}) copy-start(f32[4,512]{1,0:T(4,128)} %taps.3) | copy-start | bytes 24580
  3.6 4.4 %copy-start.20 = (f32[512]{0:T(512)S(1)}, f32[512]{0:T(512)}, u32[]{:S(2)}) copy-start(f32[512]{0:T(512)} %param.19) | copy-start | bytes 6148
  3.6 4.4 %copy-start.21 = (f32[512]{0:T(512)S(1)}, f32[512]{0:T(512)}, u32[]{:S(2)}) copy-start(f32[512]{0:T(512)} %param.14) | copy-start | bytes 6148
  3.9 4.1 %collective-permute-start.2 = (bf16[512,1024]{1,0:T(8,128)(2,1)S(1)}, bf16[512,1024]{1,0:T(8,128)(2,1)}, u32[]{:S(2)}, u32[]{:S(2)}) collective-permute-start(bf16[512,1024]{1,0:T(8,128)(2,1)S(1)} %bitcast.38), channel_id=1, source_target_pairs={{0,1},{1,0},{2,3},{3,2},{4,5},{5,4},{6,7},{7,6},{8,9},{9,8},{10,11... | collective-permute-start | bytes 3145736 | tf_op jit(solution)/shard_map/ppermute | solution.py:565
  4.4 2.8 %collective-permute-start.3 = (f32[5,512]{1,0:T(8,128)S(1)}, f32[5,512]{1,0:T(8,128)S(1)}, u32[]{:S(2)}, u32[]{:S(2)}) collective-permute-start(f32[5,512]{1,0:T(8,128)S(1)} %pad_maximum_fusion.2), channel_id=1, source_target_pairs={{0,1},{1,0},{2,3},{3,2},{4,5},{5,4},{6,7},{7,6},{8,9},{9,8},{10,11... | collective-permute-start | bytes 30728 | tf_op jit(solution)/shard_map/ppermute | solution.py:565
  6.8 36.8 %collective-permute-start = (bf16[2,512,512]{2,1,0:T(8,128)(2,1)}, bf16[2,512,512]{2,1,0:T(8,128)(2,1)}, u32[]{:S(2)}, u32[]{:S(2)}) collective-permute-start(bf16[2,512,512]{2,1,0:T(8,128)(2,1)} %constant_dynamic-slice_fusion.3), channel_id=1, source_target_pairs={{0,1},{1,0},{2,3},{3,2},{4,5},{5,4},{6,7},{7,6},{8,9},{9,8},{10,11... | collective-permute-start | bytes 3145736 | tf_op jit(solution)/shard_map/ppermute | solution.py:565
  7.3 36.4 %collective-permute-start.5 = (bf16[512,1024]{1,0:T(8,128)(2,1)S(1)}, bf16[512,1024]{1,0:T(8,128)(2,1)S(1)}, u32[]{:S(2)}, u32[]{:S(2)}) collective-permute-start(bf16[512,1024]{1,0:T(8,128)(2,1)S(1)} %copy-done.11), channel_id=1, source_target_pairs={{0,1},{1,0},{2,3},{3,2},{4,5},{5,4},{6,7},{7,6},{8,9},{9,8},{10,11... | collective-permute-start | bytes 3145736 | tf_op jit(solution)/shard_map/ppermute | solution.py:565
  7.4 36.3 %collective-permute-start.6 = (bf16[1024,512]{1,0:T(8,128)(2,1)S(1)}, bf16[1024,512]{1,0:T(8,128)(2,1)S(1)}, u32[]{:S(2)}, u32[]{:S(2)}) collective-permute-start(bf16[1024,512]{1,0:T(8,128)(2,1)S(1)} %copy-done.12), channel_id=1, source_target_pairs={{0,1},{1,0},{2,3},{3,2},{4,5},{5,4},{6,7},{7,6},{8,9},{9,8},{10,11... | collective-permute-start | bytes 3145736 | tf_op jit(solution)/shard_map/ppermute | solution.py:565
  8.0 1.0 copy-start.17
  43.7 21.0 %copy-start.14 = (bf16[1024,512]{1,0:T(8,128)(2,1)}, bf16[1024,512]{1,0:T(8,128)(2,1)S(1)}, u32[]{:S(2)}) copy-start(bf16[1024,512]{1,0:T(8,128)(2,1)S(1)} %collective-permute-done.6.down_other) | copy-start | bytes 3145732
  43.7 21.0 %copy-start.24 = (bf16[2048,512]{1,0:T(8,128)(2,1)S(1)}, bf16[2048,512]{1,0:T(8,128)(2,1)}, u32[]{:S(2)}) copy-start(bf16[2048,512]{1,0:T(8,128)(2,1)} %get-tuple-element.40.normed.left) | copy-start | bytes 6291460
  64.7 3.4 %copy-start = (bf16[2048,2048]{1,0:T(8,128)(2,1)S(1)}, bf16[2048,2048]{1,0:T(8,128)(2,1)}, u32[]{:S(2)}) copy-start(bf16[2048,2048]{1,0:T(8,128)(2,1)} %get-tuple-element.44.back_hidden.right) | copy-start | bytes 25165828
  68.1 7.7 %copy-start.18 = (bf16[512,512]{1,0:T(8,128)(2,1)S(1)}, bf16[512,512]{1,0:T(8,128)(2,1)}, u32[]{:S(2)}) copy-start(bf16[512,512]{1,0:T(8,128)(2,1)} %read_own.3) | copy-start | bytes 1572868
  74.4 1.3 copy-start.2
  75.8 25.9 %copy-start.22 = (bf16[2048,1024]{1,0:T(8,128)(2,1)S(1)}, bf16[2048,1024]{1,0:T(8,128)(2,1)}, u32[]{:S(2)}) copy-start(bf16[2048,1024]{1,0:T(8,128)(2,1)} %get-tuple-element.60.right) | copy-start | bytes 12582916
  101.7 4.0 %copy-start.23 = (bf16[2048,512]{1,0:T(8,128)(2,1)S(1)}, bf16[2048,512]{1,0:T(8,128)(2,1)}, u32[]{:S(2)}) copy-start(bf16[2048,512]{1,0:T(8,128)(2,1)} %get-tuple-element.57.left) | copy-start | bytes 6291460
  101.7 15.2 %slice-start = ((s8[8388608]{0:T(1024)(128)(4,1)}), s8[4194304]{0:T(1024)(128)(4,1)S(1)}, s32[]{:S(2)}) async-start(s8[8388608]{0:T(1024)(128)(4,1)} %bitcast.35), calls=%async_computation | async-start | bytes 8388608
  104.7 1.0 copy-start.16
  105.7 3.4 %copy-start.1 = (bf16[2048,2048]{1,0:T(8,128)(2,1)S(1)}, bf16[2048,2048]{1,0:T(8,128)(2,1)}, u32[]{:S(2)}) copy-start(bf16[2048,2048]{1,0:T(8,128)(2,1)} %get-tuple-element.48.project.right) | copy-start | bytes 25165828
  109.1 7.8 %slice-start.1 = ((s8[8388608]{0:T(1024)(128)(4,1)}), s8[4194304]{0:T(1024)(128)(4,1)S(1)}, s32[]{:S(2)}) async-start(s8[8388608]{0:T(1024)(128)(4,1)} %bitcast.35), calls=%async_computation.1 | async-start | bytes 8388608
  115.5 9.3 %copy-start.9 = (f32[512,1024]{1,0:T(8,128)}, f32[512,1024]{1,0:T(8,128)S(1)}, u32[]{:S(2)}) copy-start(f32[512,1024]{1,0:T(8,128)S(1)} %get-tuple-element.58) | copy-start | bytes 6291460
  115.5 2.9 %copy-start.6 = (bf16[2048,512]{1,0:T(8,128)(2,1)S(1)}, bf16[2048,512]{1,0:T(8,128)(2,1)}, u32[]{:S(2)}) copy-start(bf16[2048,512]{1,0:T(8,128)(2,1)} %get-tuple-element.43.tangent.left) | copy-start | bytes 6291460
  116.8 30.0 %collective-permute-start.15 = (bf16[512,1536]{1,0:T(8,128)(2,1)}, bf16[512,1536]{1,0:T(8,128)(2,1)}, u32[]{:S(2)}, u32[]{:S(2)}) collective-permute-start(bf16[512,1536]{1,0:T(8,128)(2,1)} %pad_maximum_fusion.1), channel_id=1, source_target_pairs={{0,1},{1,0},{2,3},{3,2},{4,5},{5,4},{6,7},{7,6},{8,9},{9,8},{10,11... | collective-permute-start | bytes 4718600 | tf_op jit(solution)/shard_map/ppermute | solution.py:565
  124.8 2.0 copy-start.4
  126.8 37.8 %collective-permute-start.24 = (bf16[1024,1024]{1,0:T(8,128)(2,1)}, bf16[1024,1024]{1,0:T(8,128)(2,1)}, u32[]{:S(2)}, u32[]{:S(2)}) collective-permute-start(bf16[1024,1024]{1,0:T(8,128)(2,1)} %pad_maximum_fusion), channel_id=1, source_target_pairs={{0,1},{1,0},{2,3},{3,2},{4,5},{5,4},{6,7},{7,6},{8,9},{9,8},{10,11... | collective-permute-start | bytes 6291464 | tf_op jit(solution)/shard_map/ppermute | solution.py:565
  126.9 19.9 %copy-start.10 = (f32[512,1024]{1,0:T(8,128)S(1)}, f32[512,1024]{1,0:T(8,128)}, u32[]{:S(2)}) copy-start(f32[512,1024]{1,0:T(8,128)} %copy-done.9) | copy-start | bytes 6291460
  144.8 1.3 copy-start.7
  146.1 77.3 %collective-permute-start.9 = (f32[2,512]{1,0:T(2,128)S(1)}, f32[2,512]{1,0:T(2,128)S(1)}, u32[]{:S(2)}, u32[]{:S(2)}) collective-permute-start(f32[2,512]{1,0:T(2,128)S(1)} %get-tuple-element.96), channel_id=1, source_target_pairs={{0,1},{1,0},{2,3},{3,2},{4,5},{5,4},{6,7},{7,6},{8,9},{9,8},{10,11... | collective-permute-start | bytes 12296 | tf_op jit(solution)/shard_map/ppermute | solution.py:565
  146.5 5.6 %collective-permute-start.10 = (f32[4608]{0:T(1024)S(1)}, f32[4608]{0:T(1024)S(1)}, u32[]{:S(2)}, u32[]{:S(2)}) collective-permute-start(f32[4608]{0:T(1024)S(1)} %constant_dynamic-update-slice_fusion.1), channel_id=1, source_target_pairs={{0,1},{1,0},{2,3},{3,2},{4,5},{5,4},{6,7},{7,6},{8,9},{9,8},{10,11... | collective-permute-start | bytes 55304 | tf_op jit(solution)/shard_map/ppermute | solution.py:565
  146.8 5.4 %copy-start.8 = (bf16[2048,512]{1,0:T(8,128)(2,1)S(1)}, bf16[2048,512]{1,0:T(8,128)(2,1)}, u32[]{:S(2)}) copy-start(bf16[2048,512]{1,0:T(8,128)(2,1)} %copy-done.7) | copy-start | bytes 6291460
  149.3 19.4 %collective-permute-start.16 = (bf16[256,1536]{1,0:T(8,128)(2,1)S(1)}, bf16[256,1536]{1,0:T(8,128)(2,1)S(1)}, u32[]{:S(2)}, u32[]{:S(2)}) collective-permute-start(bf16[256,1536]{1,0:T(8,128)(2,1)S(1)} %dynamic-slice_convert_fusion.1), channel_id=1, source_target_pairs={{0,2},{1,9},{2,0},{3,11},{4,6},{5,13},{6,4},{7,15},{8,10},{9,1},{1... | collective-permute-start | bytes 2359304 | tf_op jit(solution)/shard_map/ppermute | solution.py:575
  152.1 10.4 %collective-permute-start.11 = (f32[4608]{0:T(1024)S(1)}, f32[4608]{0:T(1024)S(1)}, u32[]{:S(2)}, u32[]{:S(2)}) collective-permute-start(f32[4608]{0:T(1024)S(1)} %add.115), channel_id=1, source_target_pairs={{0,2},{1,3},{2,0},{3,1},{4,6},{5,7},{6,4},{7,5},{8,10},{9,11},{10,... | collective-permute-start | bytes 55304 | tf_op jit(solution)/shard_map/ppermute | solution.py:575
  152.2 12.3 %copy-start.3 = (f32[512,1024]{1,0:T(8,128)S(1)}, f32[512,1024]{1,0:T(8,128)}, u32[]{:S(2)}) copy-start(f32[512,1024]{1,0:T(8,128)} %copy-done.2) | copy-start | bytes 6291460
  152.2 12.3 %copy-start.5 = (f32[512,1024]{1,0:T(8,128)S(1)}, f32[512,1024]{1,0:T(8,128)}, u32[]{:S(2)}) copy-start(f32[512,1024]{1,0:T(8,128)} %copy-done.4) | copy-start | bytes 6291460
  152.4 83.5 %collective-permute-start.8 = (bf16[2,512,512]{2,1,0:T(8,128)(2,1)S(1)}, bf16[2,512,512]{2,1,0:T(8,128)(2,1)}, u32[]{:S(2)}, u32[]{:S(2)}) collective-permute-start(bf16[2,512,512]{2,1,0:T(8,128)(2,1)S(1)} %get-tuple-element.83), channel_id=1, source_target_pairs={{0,1},{1,0},{2,3},{3,2},{4,5},{5,4},{6,7},{7,6},{8,9},{9,8},{10,11... | collective-permute-start | bytes 3145736 | tf_op jit(solution)/shard_map/ppermute | solution.py:565
  162.5 14.7 %collective-permute-start.12 = (f32[4608]{0:T(1024)S(1)}, f32[4608]{0:T(1024)}, u32[]{:S(2)}, u32[]{:S(2)}) collective-permute-start(f32[4608]{0:T(1024)S(1)} %add.116), channel_id=1, source_target_pairs={{0,4},{1,5},{2,6},{3,7},{4,0},{5,1},{6,2},{7,3},{8,12},{9,13},{10,... | collective-permute-start | bytes 55304 | tf_op jit(solution)/shard_map/ppermute | solution.py:575
  167.1 2.4 copy-start.13
  167.1 2.4 copy-start.15
  167.1 17.8 %collective-permute-start.25 = (bf16[512,1024]{1,0:T(8,128)(2,1)S(1)}, bf16[512,1024]{1,0:T(8,128)(2,1)}, u32[]{:S(2)}, u32[]{:S(2)}) collective-permute-start(bf16[512,1024]{1,0:T(8,128)(2,1)S(1)} %dynamic-slice_convert_fusion), channel_id=1, source_target_pairs={{0,2},{1,9},{2,0},{3,11},{4,6},{5,13},{6,4},{7,15},{8,10},{9,1},{1... | collective-permute-start | bytes 3145736 | tf_op jit(solution)/shard_map/ppermute | solution.py:575
  169.0 10.3 %collective-permute-start.17 = (bf16[128,1536]{1,0:T(8,128)(2,1)S(1)}, bf16[128,1536]{1,0:T(8,128)(2,1)S(1)}, u32[]{:S(2)}, u32[]{:S(2)}) collective-permute-start(bf16[128,1536]{1,0:T(8,128)(2,1)S(1)} %dynamic-slice_convert_fusion.3), channel_id=1, source_target_pairs={{0,4},{1,3},{2,6},{3,1},{4,0},{5,7},{6,2},{7,5},{8,12},{9,11},{10,... | collective-permute-start | bytes 1179656 | tf_op jit(solution)/shard_map/ppermute | solution.py:575
  177.9 45.5 %collective-permute-start.13 = (f32[4608]{0:T(1024)S(1)}, f32[4608]{0:T(1024)S(1)}, u32[]{:S(2)}, u32[]{:S(2)}) collective-permute-start(f32[4608]{0:T(1024)S(1)} %add.117), channel_id=1, source_target_pairs={{0,8},{1,9},{2,10},{3,11},{4,12},{5,13},{6,14},{7,15},{8,0},{9,1},... | collective-permute-start | bytes 55304 | tf_op jit(solution)/shard_map/ppermute | solution.py:575
  179.4 7.4 %collective-permute-start.18 = (bf16[64,1536]{1,0:T(8,128)(2,1)S(1)}, bf16[64,1536]{1,0:T(8,128)(2,1)S(1)}, u32[]{:S(2)}, u32[]{:S(2)}) collective-permute-start(bf16[64,1536]{1,0:T(8,128)(2,1)S(1)} %dynamic-slice_convert_fusion.5), channel_id=1, source_target_pairs={{0,8},{1,5},{2,10},{3,7},{4,12},{5,1},{6,14},{7,3},{8,0},{9,13},{1... | collective-permute-start | bytes 589832 | tf_op jit(solution)/shard_map/ppermute | solution.py:575
  186.7 12.0 %collective-permute-start.26 = (bf16[256,1024]{1,0:T(8,128)(2,1)S(1)}, bf16[256,1024]{1,0:T(8,128)(2,1)S(1)}, u32[]{:S(2)}, u32[]{:S(2)}) collective-permute-start(bf16[256,1024]{1,0:T(8,128)(2,1)S(1)} %dynamic-slice_convert_fusion.2), channel_id=1, source_target_pairs={{0,4},{1,3},{2,6},{3,1},{4,0},{5,7},{6,2},{7,5},{8,12},{9,11},{10,... | collective-permute-start | bytes 1572872 | tf_op jit(solution)/shard_map/ppermute | solution.py:575
  186.9 13.5 %collective-permute-start.19 = (bf16[32,1536]{1,0:T(8,128)(2,1)S(1)}, bf16[32,1536]{1,0:T(8,128)(2,1)S(1)}, u32[]{:S(2)}, u32[]{:S(2)}) collective-permute-start(bf16[32,1536]{1,0:T(8,128)(2,1)S(1)} %dynamic-slice_convert_fusion.7), channel_id=1, source_target_pairs={{0,16},{1,17},{2,18},{3,19},{4,20},{5,21},{6,22},{7,23},{8,24},{9,... | collective-permute-start | bytes 294920 | tf_op jit(solution)/shard_map/ppermute | solution.py:575
  199.0 7.6 %collective-permute-start.27 = (bf16[128,1024]{1,0:T(8,128)(2,1)S(1)}, bf16[128,1024]{1,0:T(8,128)(2,1)S(1)}, u32[]{:S(2)}, u32[]{:S(2)}) collective-permute-start(bf16[128,1024]{1,0:T(8,128)(2,1)S(1)} %dynamic-slice_convert_fusion.4), channel_id=1, source_target_pairs={{0,8},{1,5},{2,10},{3,7},{4,12},{5,1},{6,14},{7,3},{8,0},{9,13},{1... | collective-permute-start | bytes 786440 | tf_op jit(solution)/shard_map/ppermute | solution.py:575
  200.4 9.2 %collective-permute-start.20 = (bf16[32,1536]{1,0:T(8,128)(2,1)S(1)}, bf16[32,1536]{1,0:T(8,128)(2,1)S(1)}, u32[]{:S(2)}, u32[]{:S(2)}) collective-permute-start(bf16[32,1536]{1,0:T(8,128)(2,1)S(1)} %add_convert_fusion.1), channel_id=1, source_target_pairs={{0,16},{1,17},{2,18},{3,19},{4,20},{5,21},{6,22},{7,23},{8,24},{9,... | collective-permute-start | bytes 294920 | tf_op jit(solution)/shard_map/ppermute | solution.py:575
  206.7 7.4 %collective-permute-start.28 = (bf16[64,1024]{1,0:T(8,128)(2,1)S(1)}, bf16[64,1024]{1,0:T(8,128)(2,1)S(1)}, u32[]{:S(2)}, u32[]{:S(2)}) collective-permute-start(bf16[64,1024]{1,0:T(8,128)(2,1)S(1)} %dynamic-slice_convert_fusion.6), channel_id=1, source_target_pairs={{0,16},{1,17},{2,18},{3,19},{4,20},{5,21},{6,22},{7,23},{8,24},{9,... | collective-permute-start | bytes 393224 | tf_op jit(solution)/shard_map/ppermute | solution.py:575
  209.6 6.3 %collective-permute-start.21 = (bf16[64,1536]{1,0:T(8,128)(2,1)S(1)}, bf16[64,1536]{1,0:T(8,128)(2,1)S(1)}, u32[]{:S(2)}, u32[]{:S(2)}) collective-permute-start(bf16[64,1536]{1,0:T(8,128)(2,1)S(1)} %maximum_select_fusion.9), channel_id=1, source_target_pairs={{0,8},{1,5},{2,10},{3,7},{4,12},{5,1},{6,14},{7,3},{8,0},{9,13},{1... | collective-permute-start | bytes 589832 | tf_op jit(solution)/shard_map/ppermute | solution.py:575
  214.2 7.3 %collective-permute-start.29 = (bf16[64,1024]{1,0:T(8,128)(2,1)S(1)}, bf16[64,1024]{1,0:T(8,128)(2,1)S(1)}, u32[]{:S(2)}, u32[]{:S(2)}) collective-permute-start(bf16[64,1024]{1,0:T(8,128)(2,1)S(1)} %add_convert_fusion), channel_id=1, source_target_pairs={{0,16},{1,17},{2,18},{3,19},{4,20},{5,21},{6,22},{7,23},{8,24},{9,... | collective-permute-start | bytes 393224 | tf_op jit(solution)/shard_map/ppermute | solution.py:575
  216.0 15.6 %collective-permute-start.22 = (bf16[128,1536]{1,0:T(8,128)(2,1)S(1)}, bf16[128,1536]{1,0:T(8,128)(2,1)}, u32[]{:S(2)}, u32[]{:S(2)}) collective-permute-start(bf16[128,1536]{1,0:T(8,128)(2,1)S(1)} %maximum_select_fusion.7), channel_id=1, source_target_pairs={{0,4},{1,3},{2,6},{3,1},{4,0},{5,7},{6,2},{7,5},{8,12},{9,11},{10,... | collective-permute-start | bytes 1179656 | tf_op jit(solution)/shard_map/ppermute | solution.py:575
  222.2 7.3 %collective-permute-start.30 = (bf16[128,1024]{1,0:T(8,128)(2,1)}, bf16[128,1024]{1,0:T(8,128)(2,1)}, u32[]{:S(2)}, u32[]{:S(2)}) collective-permute-start(bf16[128,1024]{1,0:T(8,128)(2,1)} %maximum_select_fusion.8), channel_id=1, source_target_pairs={{0,8},{1,5},{2,10},{3,7},{4,12},{5,1},{6,14},{7,3},{8,0},{9,13},{1... | collective-permute-start | bytes 786440 | tf_op jit(solution)/shard_map/ppermute | solution.py:575
  223.4 19.5 %collective-permute-start.7 = (bf16[2,512,512]{2,1,0:T(8,128)(2,1)}, bf16[2,512,512]{2,1,0:T(8,128)(2,1)}, u32[]{:S(2)}, u32[]{:S(2)}) collective-permute-start(bf16[2,512,512]{2,1,0:T(8,128)(2,1)} %get-tuple-element.85), channel_id=1, source_target_pairs={{0,1},{1,0},{2,3},{3,2},{4,5},{5,4},{6,7},{7,6},{8,9},{9,8},{10,11... | collective-permute-start | bytes 3145736 | tf_op jit(solution)/shard_map/ppermute | solution.py:565
  223.4 4.9 %collective-permute-start.14 = (f32[4608]{0:T(1024)S(1)}, f32[4608]{0:T(1024)S(1)}, u32[]{:S(2)}, u32[]{:S(2)}) collective-permute-start(f32[4608]{0:T(1024)S(1)} %add.118), channel_id=1, source_target_pairs={{0,16},{1,17},{2,18},{3,19},{4,20},{5,21},{6,22},{7,23},{8,24},{9,... | collective-permute-start | bytes 55304 | tf_op jit(solution)/shard_map/ppermute | solution.py:575
  231.0 9.2 %collective-permute-start.31 = (bf16[256,1024]{1,0:T(8,128)(2,1)S(1)}, bf16[256,1024]{1,0:T(8,128)(2,1)S(1)}, u32[]{:S(2)}, u32[]{:S(2)}) collective-permute-start(bf16[256,1024]{1,0:T(8,128)(2,1)S(1)} %maximum_select_fusion.6), channel_id=1, source_target_pairs={{0,4},{1,3},{2,6},{3,1},{4,0},{5,7},{6,2},{7,5},{8,12},{9,11},{10,... | collective-permute-start | bytes 1572872 | tf_op jit(solution)/shard_map/ppermute | solution.py:575
  232.9 15.0 %collective-permute-start.23 = (bf16[256,1536]{1,0:T(8,128)(2,1)S(1)}, bf16[256,1536]{1,0:T(8,128)(2,1)S(1)}, u32[]{:S(2)}, u32[]{:S(2)}) collective-permute-start(bf16[256,1536]{1,0:T(8,128)(2,1)S(1)} %maximum_select_fusion.5), channel_id=1, source_target_pairs={{0,2},{1,9},{2,0},{3,11},{4,6},{5,13},{6,4},{7,15},{8,10},{9,1},{1... | collective-permute-start | bytes 2359304 | tf_op jit(solution)/shard_map/ppermute | solution.py:575
  240.7 18.6 %collective-permute-start.32 = (bf16[512,1024]{1,0:T(8,128)(2,1)S(1)}, bf16[512,1024]{1,0:T(8,128)(2,1)}, u32[]{:S(2)}, u32[]{:S(2)}) collective-permute-start(bf16[512,1024]{1,0:T(8,128)(2,1)S(1)} %maximum_select_fusion.4), channel_id=1, source_target_pairs={{0,2},{1,9},{2,0},{3,11},{4,6},{5,13},{6,4},{7,15},{8,10},{9,1},{1... | collective-permute-start | bytes 3145736 | tf_op jit(solution)/shard_map/ppermute | solution.py:575
  (1 other events, 0.6 us)
